TPU v7x, 32 devices: a whole 2x2x4 slice. The times are simulated.
32 devices in a mesh: seq: 8 (over z, y), grp: 4 (over x, core).
Axes of the slice: x: 2, y: 2, z: 4, core: 2. Of those that a mesh axis runs over, the one named last changes fastest.
Arguments:
- queries: bfloat16 [8, 4096], P('seq'), may hold values from -6 to 6
- prompt_keys: bfloat16 [32768, 512], P(('seq', 'grp')), may hold values from -15 to 15
- prompt_values: bfloat16 [32768, 512], P(('seq', 'grp')), may hold values from -6 to 6
- suffix_keys: bfloat16 [8, 1024, 512], P('seq', 'grp'), may hold values from -16 to 16
- suffix_values: bfloat16 [8, 1024, 512], P('seq', 'grp'), may hold values from -6 to 6
- lengths: int32 [8], P('seq'), may hold values from 1 to 1024, as said below
Outputs:
- attended: bfloat16 [8, 4096], P('seq', 'grp')
Inputs may be any that keep to these rules, and one draw needn't show every extreme that they name: `lengths`: some response has exactly 1024 live positions.
All inputs are finite; a program needn't handle non-finite values.
Results may differ from a plain program's by a relative error of at most 0.003.
Values may be sent and summed in bfloat16 or wider, within the bound.
No kernel may reach another device: no remote copies, remote signals or barrier semaphores. Data moves between devices by JAX's collectives and lax.ppermute only.
A program may use at most 64 MiB of HBM per device.

v0:
```python
import math

import jax
import jax.numpy as jnp
from jax import lax
from jax.sharding import PartitionSpec as P

Q_HEADS = 32
KV_HEADS = 4
HEAD_DIM = 128
GROUP = 8


def head_section(outputs, totals, peaks):
    outputs, totals = (
        lax.psum_scatter(outputs, "grp", scatter_dimension=1, tiled=True),
        lax.psum_scatter(totals, "grp", scatter_dimension=1, tiled=True),
    )
    width = totals.shape[1]
    peaks = lax.dynamic_slice_in_dim(peaks, lax.axis_index("grp") * width, width, 1)
    return (outputs, totals, peaks)


def response_section(outputs, totals, peaks):
    outputs, totals = (
        lax.psum_scatter(outputs, "seq", scatter_dimension=0, tiled=True),
        lax.psum_scatter(totals, "seq", scatter_dimension=0, tiled=True),
    )
    height = totals.shape[0]
    peaks = lax.dynamic_slice_in_dim(peaks, lax.axis_index("seq") * height, height, 0)
    return (outputs, totals, peaks)


def on_device(queries, prompt_keys, prompt_values, suffix_keys, suffix_values, lengths):
    scale = 1.0 / math.sqrt(HEAD_DIM)
    every = lax.all_gather(queries, "seq", axis=0, tiled=True)
    count = every.shape[0]
    grouped = every.reshape(count, KV_HEADS, GROUP, HEAD_DIM)

    def one_head(index):
        query_part = lax.dynamic_index_in_dim(grouped, index, 1, keepdims=False).reshape(
            count * GROUP, HEAD_DIM
        )
        key_part = lax.dynamic_slice_in_dim(prompt_keys, index * HEAD_DIM, HEAD_DIM, 1)
        value_part = lax.dynamic_slice_in_dim(prompt_values, index * HEAD_DIM, HEAD_DIM, 1)
        scores = (
            lax.dot_general(
                query_part, key_part, (((1,), (1,)), ((), ())), preferred_element_type=jnp.float32
            )
            * scale
        )
        peak = jnp.max(scores, axis=1)
        expo = jnp.exp(scores - peak[:, None])
        total = jnp.sum(expo, axis=1)
        output = jnp.dot(expo.astype(jnp.bfloat16), value_part, preferred_element_type=jnp.float32)
        return (peak, total, output)

    head_peaks, head_totals, head_outputs = lax.map(one_head, jnp.arange(KV_HEADS))
    peaks = head_peaks.reshape(KV_HEADS, count, GROUP).transpose(1, 0, 2).reshape(count, Q_HEADS)
    totals = head_totals.reshape(KV_HEADS, count, GROUP).transpose(1, 0, 2).reshape(count, Q_HEADS)
    outputs = (
        head_outputs.reshape(KV_HEADS, count, GROUP, HEAD_DIM)
        .transpose(1, 0, 2, 3)
        .reshape(count, Q_HEADS, HEAD_DIM)
    )
    own_rows = queries.shape[0]
    own_span = suffix_keys.shape[1]
    own_query = queries.reshape(own_rows, KV_HEADS, GROUP, HEAD_DIM)
    own_keys = suffix_keys.reshape(own_rows, own_span, KV_HEADS, HEAD_DIM)
    own_values = suffix_values.reshape(own_rows, own_span, KV_HEADS, HEAD_DIM)
    own_scores = (
        jnp.einsum("rjgd,rtjd->rjgt", own_query, own_keys, preferred_element_type=jnp.float32)
        * scale
    )
    position = lax.axis_index("grp") * own_span + jnp.arange(own_span, dtype=jnp.int32)
    live = (position[None, :] < lengths[:, None])[:, None, None, :]
    masked = jnp.where(live, own_scores, -1e30)
    own_peak = jnp.max(masked, axis=-1)
    own_expo = jnp.where(live, jnp.exp(masked - own_peak[..., None]), 0.0)
    own_total = jnp.sum(own_expo, axis=-1).reshape(own_rows, Q_HEADS)
    own_output = jnp.einsum(
        "rjgt,rtjd->rjgd",
        own_expo.astype(jnp.bfloat16),
        own_values,
        preferred_element_type=jnp.float32,
    ).reshape(own_rows, Q_HEADS, HEAD_DIM)
    own_peak = own_peak.reshape(own_rows, Q_HEADS)
    first = lax.axis_index("seq") * own_rows
    base_peak = lax.dynamic_slice_in_dim(peaks, first, own_rows, 0)
    base_total = lax.dynamic_slice_in_dim(totals, first, own_rows, 0)
    base_output = lax.dynamic_slice_in_dim(outputs, first, own_rows, 0)
    joined = jnp.maximum(base_peak, own_peak)
    base_factor = jnp.exp(base_peak - joined)
    own_factor = jnp.exp(own_peak - joined)
    joined_total = base_total * base_factor + own_total * own_factor
    joined_output = base_output * base_factor[..., None] + own_output * own_factor[..., None]
    peaks = lax.dynamic_update_slice_in_dim(peaks, joined, first, 0)
    totals = lax.dynamic_update_slice_in_dim(totals, joined_total, first, 0)
    outputs = lax.dynamic_update_slice_in_dim(outputs, joined_output, first, 0)
    highest = lax.pmax(peaks, ("seq", "grp"))
    factor = jnp.exp(peaks - highest)
    outputs = outputs * factor[:, :, None]
    totals = totals * factor
    peaks = highest
    outputs, totals, peaks = head_section(outputs, totals, peaks)
    outputs, totals, peaks = response_section(outputs, totals, peaks)
    result = outputs / totals[:, :, None]
    return result.reshape(result.shape[0], result.shape[1] * HEAD_DIM).astype(jnp.bfloat16)


def solution(mesh):
    in_specs = (
        P("seq", None),
        P(("seq", "grp"), None),
        P(("seq", "grp"), None),
        P("seq", "grp", None),
        P("seq", "grp", None),
        P("seq"),
    )
    out_specs = P("seq", "grp")
    return jax.shard_map(
        on_device, mesh=mesh, in_specs=in_specs, out_specs=out_specs, check_vma=False
    )
```

profile of v0, /device:TPU:0, one launch (start us, length us, event | category | flops | bytes accessed | tf_op | source)
XLA Modules:
  0.0 173.3 jit_solution(9564515317729132454)
XLA Ops:
  6.5 32.6 %all-gather = bf16[8,1,4096]{2,1,0:T(2,128)(2,1)S(1)} all-gather(bf16[1,1,4096]{2,1,0:T(2,128)(2,1)} %bitcast.74), channel_id=1, replica_groups=mesh['seq'=8,'grp'=4] {'seq'}, dimensions={0}, use_global_device_ids=true | all-gather | bytes 73728 | tf_op jit(solution)/shard_map/all_gather | solution.py:36
  39.7 24.8 %while.14 = (s32[]{:T(128)}, f32[4,64]{1,0:T(4,128)S(1)}, f32[4,64]{1,0:T(4,128)S(1)}, f32[4,64,128]{2,1,0:T(8,128)S(1)}, s32[4]{0:T(128)S(1)}, /*index=5*/bf16[...) while((s32[]{:T(128)}, f32[4,64]{1,0:T(4,128)S(1)}, ...), condition=%wide.region_3.4_spmd, body=%wide.region_0.3_spmd.sunk | while | flops 33947528 | bytes 1362425 | solution.py:58
  39.7 0.7 dynamic_slice.61
  43.1 1.3 fusion.45
  44.7 1.2 fusion.47
  45.9 0.7 dynamic_slice.61
  49.3 1.3 fusion.45
  50.9 1.2 fusion.47
  52.1 0.7 dynamic_slice.61
  55.5 1.3 fusion.45
  57.1 1.2 fusion.47
  58.3 0.7 dynamic_slice.61
  61.7 1.3 fusion.45
  63.3 1.2 fusion.47
  66.3 39.6 %pmax.7 = f32[8,32]{1,0:T(8,128)S(1)} all-reduce(f32[8,32]{1,0:T(8,128)S(1)} %dynamic_update_slice.21), channel_id=1, replica_groups=mesh['seq'=8,'grp'=4] {'seq','grp'}, use_global_device_ids=true, to_apply=%region_5.6 | all-reduce | flops 256 | bytes 2048 | tf_op jit(solution)/shard_map/pmax | solution.py:100
  106.3 0.7 broadcast_multiply_fusion
  107.0 0.6 copy-done.4
  108.3 0.6 dynamic-slice
  109.6 5.8 %all-reduce.1 = f32[8,32]{1,0:T(8,128)S(1)} all-reduce(f32[8,32]{1,0:T(8,128)S(1)} %get-tuple-element.72), channel_id=4, replica_groups=mesh['seq'=8,'grp'=4] {'grp'}, use_global_device_ids=true, to_apply=%region_9.10.clone | all-reduce | flops 256 | bytes 2048
  115.5 11.6 %reduce-scatter.3.cloned.1.call-done = f32[8,8,128]{2,1,0:T(8,128)} async-done(((f32[8,32,128]{2,1,0:T(8,128)}), f32[8,8,128]{2,1,0:T(8,128)}) %reduce-scatter.3.cloned.1.call-update) | async-done | bytes 32784 | tf_op jit(solution)/shard_map/reduce_scatter | solution.py:16
  127.2 37.4 %all-reduce.3 = (f32[8,8]{1,0:T(8,128)S(1)}, f32[8,8,128]{2,1,0:T(8,128)S(1)}) all-reduce(f32[8,8]{1,0:T(8,128)S(1)} %constant_dynamic-slice_fusion.1, f32[8,8,128]{2,1,0:T(8,128)} %reduce-scatter.3.cloned.1.call-done), channel_id=5, replica_groups=mesh['seq'=8,'grp'=4] {'seq'}, use_global_device_ids=true, to_apply=%region_10.11.clone | all-reduce | flops 8256 | bytes 66048
  164.6 0.6 fusion.28
  165.2 0.7 fusion.25
  165.9 0.6 copy.40
  (52 shorter events, 3.7 us)
Async XLA Ops:
  6.5 120.6 %reduce-scatter.3.cloned.1.call-start = ((), (), s32[]{:S(2)}) async-start(), calls=%async_computation.1 | async-start | bytes 163840 | tf_op jit(solution)/shard_map/reduce_scatter | solution.py:16
  6.5 32.6 %copy-start.2 = (bf16[1,4096]{1,0:T(2,128)(2,1)S(1)}, bf16[1,4096]{1,0:T(2,128)(2,1)}, u32[]{:S(2)}) copy-start(bf16[1,4096]{1,0:T(2,128)(2,1)} %param.8) | copy-start | bytes 24580
  39.6 25.0 %copy-start = (bf16[1,256,512]{2,1,0:T(8,128)(2,1)S(1)}, bf16[1,256,512]{2,1,0:T(8,128)(2,1)}, u32[]{:S(2)}) copy-start(bf16[1,256,512]{2,1,0:T(8,128)(2,1)} %param.11) | copy-start | bytes 786436
  65.7 40.3 %copy-start.1 = (bf16[1,256,512]{2,1,0:T(8,128)(2,1)S(1)}, bf16[1,256,512]{2,1,0:T(8,128)(2,1)}, u32[]{:S(2)}) copy-start(bf16[1,256,512]{2,1,0:T(8,128)(2,1)} %param.12) | copy-start | bytes 786436
  107.0 0.7 copy-start.4
  107.7 0.7 copy-start.3
Sparse Core Ops, SparseCore 0:
  107.2 19.9 reduce-scatter.2
where the time goes:
time: 174 us; the launch traced here: 173 us
  blocking collectives  116 us (67%)
  between operations  14.8 us (9%)
  waiting for transfers between devices  11.6 us (7%)
  loops' own time  11.2 us (6%)
  matrix products  10.3 us (6%)
  local copies, waits for them, and re-layouts  6.98 us (4%)
  other arithmetic  2.91 us (2%)
    unnamed x2, blocking collectives  43.2 us
    pmax x1, blocking collectives, on_device(): highest = lax.pmax(peaks, ('seq', 'grp'))  39.6 us
    all_gather x1, blocking collectives, on_device(): every = lax.all_gather(queries, 'seq', axis=0, tiled=True)  32.6 us
    reduce_scatter x1, waiting for transfers between devices, head_section(): lax.psum_scatter(outputs, 'grp', scatter_dimension=1, tiled=True)  11.6 us
    another operation x1, loops' own time, on_device(): lax.map(one_head, jnp.arange(KV_HEADS))  11.2 us
    dot_general x4, matrix products, one_head(): lax.dot_general(query_part, key_part, (((1,), (1,)), ((), ())), preferred...  5.08 us
    dot_general x4, matrix products, one_head(): jnp.dot(expo.astype(jnp.bfloat16), value_part, preferred_element_type=jnp...  4.77 us
  transfers between devices with their start and end apart: 1, of which 1 were waited for; matrix products, arithmetic and copies ran while one was open for 1% of the time, Pallas kernels for 0%

commit v1 on v0

v1 whole, which is shorter than its diff:
```python
import functools
import math

import jax
import jax.numpy as jnp
from jax import lax
from jax.experimental import pallas as pl
from jax.experimental.pallas import tpu as pltpu
from jax.sharding import PartitionSpec as P

Q_HEADS = 32
KV_HEADS = 4
HEAD_DIM = 128
GROUP = 8
BLOCK = 8
ROWS = GROUP + 1
WIDTH = ROWS * HEAD_DIM
LOG2_SCALE = math.log2(math.e) / math.sqrt(HEAD_DIM)
LOWEST = -1e30

VMEM = pl.BlockSpec(memory_space=pltpu.VMEM)
SMEM = pl.BlockSpec(memory_space=pltpu.SMEM)


def in_vmem(x):
    return pltpu.with_memory_space_constraint(x, pltpu.VMEM)


def spread_kernel(query_ref, out_ref):
    query = query_ref[...].astype(jnp.float32)
    rows = [query[:, h * HEAD_DIM : (h + 1) * HEAD_DIM] for h in range(Q_HEADS)]
    rows = jnp.concatenate(rows, axis=0).astype(out_ref.dtype)
    out_ref[...] = jnp.broadcast_to(rows[None], out_ref.shape)


def dot_rows(a, b):
    return lax.dot_general(a, b, (((1,), (1,)), ((), ())), preferred_element_type=jnp.float32)


def partial_kernel(lengths_ref, query_ref, key_ref, value_ref, own_key_ref, own_value_ref, out_ref):
    count = query_ref.shape[0]
    span = own_key_ref.shape[0]
    me = lax.axis_index("seq")
    position = lax.axis_index("grp") * span + lax.broadcasted_iota(jnp.int32, (GROUP, span), 1)
    live = position < lengths_ref[0]
    own_query = query_ref[me].astype(jnp.float32)
    chunks = out_ref.reshape(out_ref.shape[0] * ROWS, HEAD_DIM)

    own = []
    for j in range(KV_HEADS):
        columns = slice(j * HEAD_DIM, (j + 1) * HEAD_DIM)
        query = own_query[j * GROUP : (j + 1) * GROUP].astype(jnp.bfloat16)
        scores = jnp.where(live, dot_rows(query, own_key_ref[:, columns]), LOWEST)
        peak = jnp.max(scores, axis=1, keepdims=True)
        expo = jnp.where(live, jnp.exp2((scores - peak) * LOG2_SCALE), 0.0)
        total = jnp.sum(expo, axis=1, keepdims=True)
        output = jnp.dot(
            expo.astype(jnp.bfloat16), own_value_ref[:, columns], preferred_element_type=jnp.float32
        )
        own.append((peak, total, output))

    def one_block(block):
        queries = query_ref[pl.ds(block * BLOCK, BLOCK)].astype(jnp.float32)
        response = block * BLOCK + lax.broadcasted_iota(jnp.int32, (BLOCK, GROUP, 1), 0)
        mine = response == me
        lane = lax.broadcasted_iota(jnp.int32, (BLOCK * GROUP, HEAD_DIM), 1)
        peaks = jnp.zeros((BLOCK * GROUP, HEAD_DIM), jnp.float32)
        totals = jnp.zeros((BLOCK * GROUP, HEAD_DIM), jnp.float32)
        for j in range(KV_HEADS):
            columns = slice(j * HEAD_DIM, (j + 1) * HEAD_DIM)
            query = queries[:, j * GROUP : (j + 1) * GROUP].reshape(BLOCK * GROUP, HEAD_DIM)
            scores = dot_rows(query.astype(jnp.bfloat16), key_ref[:, columns])
            peak = jnp.max(scores, axis=1, keepdims=True)
            expo = jnp.exp2((scores - peak) * LOG2_SCALE)
            total = jnp.sum(expo, axis=1, keepdims=True)
            output = jnp.dot(
                expo.astype(jnp.bfloat16), value_ref[:, columns], preferred_element_type=jnp.float32
            )
            own_peak, own_total, own_output = own[j]
            peak = peak.reshape(BLOCK, GROUP, 1)
            total = total.reshape(BLOCK, GROUP, 1)
            output = output.reshape(BLOCK, GROUP, HEAD_DIM)
            joined = jnp.where(mine, jnp.maximum(peak, own_peak[None]), peak)
            factor = jnp.exp2((peak - joined) * LOG2_SCALE)
            own_factor = jnp.where(mine, jnp.exp2((own_peak[None] - joined) * LOG2_SCALE), 0.0)
            total = total * factor + own_total[None] * own_factor
            output = output * factor + own_output[None] * own_factor
            peaks = jnp.where(lane == j, joined.reshape(BLOCK * GROUP, 1), peaks)
            totals = jnp.where(lane == j, total.reshape(BLOCK * GROUP, 1), totals)
            for r in range(BLOCK):
                chunk = ((block * BLOCK + r) * KV_HEADS + j) * ROWS
                chunks[pl.ds(chunk, GROUP), :] = output[r]
        sums = jnp.concatenate([peaks, totals], axis=0).T
        for r in range(BLOCK):
            for j in range(KV_HEADS):
                chunk = ((block * BLOCK + r) * KV_HEADS + j) * ROWS
                chunks[pl.ds(chunk + GROUP, 1), :] = sums[j : j + 1]

    if count == BLOCK:
        one_block(0)
    else:
        pl.loop(0, count // BLOCK)(one_block)


def join_kernel(parts_ref, out_ref):
    parts = parts_ref.shape[0]
    chunks = parts_ref.reshape(parts * ROWS, HEAD_DIM)
    sums = parts_ref[:, 0, GROUP * HEAD_DIM :]
    offset = (lax.axis_index("seq") % BLOCK) * GROUP
    sums = pltpu.roll(sums, (HEAD_DIM - offset) % HEAD_DIM, 1).T
    peaks = sums[:GROUP]
    totals = sums[BLOCK * GROUP : BLOCK * GROUP + GROUP]
    factor = jnp.exp2((peaks - jnp.max(peaks, axis=1, keepdims=True)) * LOG2_SCALE)
    total = jnp.sum(factor * totals, axis=1, keepdims=True)
    acc = [jnp.zeros((GROUP, HEAD_DIM), jnp.float32)] * 4
    for i in range(parts):
        acc[i % 4] += factor[:, i : i + 1] * chunks[i * ROWS : i * ROWS + GROUP, :]
    output = ((acc[0] + acc[1]) + (acc[2] + acc[3])) / total
    for h in range(GROUP):
        out_ref[:, h * HEAD_DIM : (h + 1) * HEAD_DIM] = output[h : h + 1].astype(out_ref.dtype)


def on_device(seq, grp, queries, prompt_keys, prompt_values, suffix_keys, suffix_values, lengths):
    copies = pl.pallas_call(
        spread_kernel,
        out_shape=pltpu.VMEM((seq, Q_HEADS, HEAD_DIM), queries.dtype),
        in_specs=[VMEM],
        out_specs=VMEM,
    )(queries)
    every = lax.all_to_all(copies, "seq", 0, 0, tiled=True)
    span = suffix_keys.shape[1]
    width = KV_HEADS * HEAD_DIM
    partial = pl.pallas_call(
        partial_kernel,
        out_shape=pltpu.VMEM((seq * grp, 1, WIDTH), jnp.float32),
        in_specs=[SMEM] + [VMEM] * 5,
        out_specs=VMEM,
    )(
        lengths,
        in_vmem(every),
        in_vmem(prompt_keys),
        in_vmem(prompt_values),
        in_vmem(suffix_keys.reshape(span, width)),
        in_vmem(suffix_values.reshape(span, width)),
    )
    parts = lax.all_to_all(partial, ("seq", "grp"), 0, 0, tiled=True)
    return pl.pallas_call(
        join_kernel,
        out_shape=jax.ShapeDtypeStruct((1, GROUP * HEAD_DIM), queries.dtype),
        in_specs=[VMEM],
        out_specs=VMEM,
    )(in_vmem(parts))


def solution(mesh):
    in_specs = (
        P("seq", None),
        P(("seq", "grp"), None),
        P(("seq", "grp"), None),
        P("seq", "grp", None),
        P("seq", "grp", None),
        P("seq"),
    )
    return jax.shard_map(
        functools.partial(on_device, mesh.shape["seq"], mesh.shape["grp"]),
        mesh=mesh,
        in_specs=in_specs,
        out_specs=P("seq", "grp"),
        check_vma=False,
    )
```

time: 174 us -> 34 us (0.20)
  blocking collectives: 116 us -> 10.3 us
  between operations: 14.8 us -> 0.67 us
  loops' own time: 11.2 us -> 0 us
  matrix products: 10.3 us -> 0 us
  starting transfers between devices: 0.01 us -> 7.28 us
  waiting for transfers between devices: 11.6 us -> 6.25 us
  Pallas kernels: 0 us -> 4.7 us
  other arithmetic: 2.91 us -> 0 us
  local copies, waits for them, and re-layouts: 6.98 us -> 4.35 us
    unnamed x2 -> x0, blocking collectives: 43.2 us -> none
    pmax x1 -> x0, blocking collectives: 39.6 us -> none  [on_device(): highest = lax.pmax(peaks, ('seq', 'grp'))]
    all_gather x1 -> x0, blocking collectives: 32.6 us -> none  [on_device(): every = lax.all_gather(queries, 'seq', axis=0, tiled=True)]
    reduce_scatter x1 -> x0, waiting for transfers between devices: 11.6 us -> none  [head_section(): lax.psum_scatter(outputs, 'grp', scatter_dimension=1, tiled=True)]
    another operation x1 -> x0, loops' own time: 11.2 us -> none  [on_device(): lax.map(one_head, jnp.arange(KV_HEADS))]
    all_to_all x0 -> x1, blocking collectives: none -> 10.3 us  [on_device(): parts = lax.all_to_all(partial, ('seq', 'grp'), 0, 0, tiled=True)]
    dot_general x10 -> x0, matrix products: 10.3 us -> none  [the longest x4 5.08 us: one_head(): lax.dot_general(query_part, key_part, (((1,), (1,)), ((), ())), preferred...]
    all_to_all x0 -> x1, starting transfers between devices: none -> 7.28 us  [on_device(): every = lax.all_to_all(copies, 'seq', 0, 0, tiled=True)]
  transfers between devices with their start and end apart: 1 -> 1, of which waited for: 1 -> 1; matrix products, arithmetic and copies ran while one was open for 1% -> 0% of each run, Pallas kernels for 0% -> 0%
where the time goes in v1:
time: 34 us; the launch traced here: 33.6 us
  blocking collectives  10.3 us (30%)
  starting transfers between devices  7.28 us (21%)
  waiting for transfers between devices  6.25 us (18%)
  Pallas kernels  4.7 us (14%)
  local copies, waits for them, and re-layouts  4.35 us (13%)
  between operations  0.67 us (2%)
    all_to_all x1, blocking collectives, on_device(): parts = lax.all_to_all(partial, ('seq', 'grp'), 0, 0, tiled=True)  10.3 us
    all_to_all x1, starting transfers between devices, on_device(): every = lax.all_to_all(copies, 'seq', 0, 0, tiled=True)  7.28 us
    all_to_all x1, waiting for transfers between devices, on_device(): every = lax.all_to_all(copies, 'seq', 0, 0, tiled=True)  6.25 us
    unnamed x8, local copies, waits for them, and re-layouts  4.35 us
    pallas_call x1, Pallas kernels, on_device(): pl.pallas_call(partial_kernel, out_shape=pltpu.VMEM((seq * grp, 1, WIDTH)...  2.36 us
    pallas_call x1, Pallas kernels, on_device(): pl.pallas_call(spread_kernel, out_shape=pltpu.VMEM((seq, Q_HEADS, HEAD_DI...  1.35 us
    pallas_call x1, Pallas kernels, on_device(): pl.pallas_call(join_kernel, out_shape=jax.ShapeDtypeStruct((1, GROUP * HE...  1 us
  transfers between devices with their start and end apart: 1, of which 1 were waited for; matrix products, arithmetic and copies ran while one was open for 0% of the time, Pallas kernels for 0%

profile of v1, /device:TPU:0, one launch (start us, length us, event | category | flops | bytes accessed | tf_op | source)
XLA Modules:
  0.0 33.6 jit_solution(12391553833580633648)
XLA Ops:
  0.0 1.3 %shard_map.64 = bf16[8,32,128]{2,1,0:T(8,128)(2,1)} custom-call(bf16[1,4096]{1,0:T(2,128)(2,1)} %query_ref.1), custom_call_target="tpu_custom_call" | custom-call | tf_op jit(solution)/shard_map/pallas_call | solution.py:124
  1.3 7.3 %all-to-all-start = ((bf16[8,32,128]{2,1,0:T(8,128)(2,1)}), bf16[8,32,128]{2,1,0:T(8,128)(2,1)S(1)}, u32[]{:S(2)}, u32[]{:S(2)}) async-start(bf16[8,32,128]{2,1,0:T(8,128)(2,1)} %shard_map.64), calls=%async_computation | async-start | bytes 131072 | tf_op jit(solution)/shard_map/all_to_all | solution.py:130
  9.3 6.3 %all-to-all-done.query_ref = bf16[8,32,128]{2,1,0:T(8,128)(2,1)S(1)} async-done(((bf16[8,32,128]{2,1,0:T(8,128)(2,1)}), bf16[8,32,128]{2,1,0:T(8,128)(2,1)S(1)}, u32[]{:S(2)}, u32[]{:S(2)}) %all-to-all-start) | async-done | bytes 65568 | tf_op jit(solution)/shard_map/all_to_all | solution.py:130
  15.5 0.0 copy-start
  15.5 1.2 %copy-done = bf16[1024,512]{1,0:T(8,128)(2,1)S(1)} copy-done((bf16[1024,512]{1,0:T(8,128)(2,1)S(1)}, bf16[1024,512]{1,0:T(8,128)(2,1)}, u32[]{:S(2)}) %copy-start) | copy-done | bytes 1048600
  16.8 0.0 copy-start.1
  16.8 1.2 %copy-done.1 = bf16[1024,512]{1,0:T(8,128)(2,1)S(1)} copy-done((bf16[1024,512]{1,0:T(8,128)(2,1)S(1)}, bf16[1024,512]{1,0:T(8,128)(2,1)}, u32[]{:S(2)}) %copy-start.1) | copy-done | bytes 1048600
  18.0 0.0 copy-start.2
  18.0 0.9 %copy-done.2 = bf16[1,256,512]{2,1,0:T(8,128)(2,1)S(1)} copy-done((bf16[1,256,512]{2,1,0:T(8,128)(2,1)S(1)}, bf16[1,256,512]{2,1,0:T(8,128)(2,1)}, u32[]{:S(2)}) %copy-start.2) | copy-done | bytes 262168
  18.9 0.0 copy-start.3
  18.9 0.9 %copy-done.3 = bf16[1,256,512]{2,1,0:T(8,128)(2,1)S(1)} copy-done((bf16[1,256,512]{2,1,0:T(8,128)(2,1)S(1)}, bf16[1,256,512]{2,1,0:T(8,128)(2,1)}, u32[]{:S(2)}) %copy-start.3) | copy-done | bytes 262168
  19.9 2.4 %shard_map.65 = f32[32,1,1152]{2,1,0:T(1,128)S(1)} custom-call(s32[1]{0:T(128)S(6)} %copy.7.lengths_ref, bf16[8,32,128]{2,1,0:T(8,128)(2,1)S(1)} %all-to-all-done.query_ref, bf16[1024,512]{1,0:T(8,128)(2,1)S(1)} %copy-done, bf16[1024,512]{1,0:T(8,128)(2,1)S(1)} %copy-done.1, bf16[256,512]{1,0:T(8,128)(2,1)S(1)} %bitcast.2, bf16[256,512]{1,0:T(8,128)(2,1)S(1)} %bitcast.3), custom_call_target="tpu_custom_call" | custom-call | tf_op jit(solution)/shard_map/pallas_call | solution.py:133
  22.3 10.3 %all_to_all.10.parts_ref = f32[32,1,1152]{2,1,0:T(1,128)S(1)} all-to-all(f32[32,1,1152]{2,1,0:T(1,128)S(1)} %shard_map.65), channel_id=1, replica_groups=mesh['seq'=8,'grp'=4] {'seq','grp'}, dimensions={0} | all-to-all | bytes 294912 | tf_op jit(solution)/shard_map/all_to_all | solution.py:146
  32.6 1.0 %shard_map.66 = bf16[1,1024]{1,0:T(2,128)(2,1)} custom-call(f32[32,1,1152]{2,1,0:T(1,128)S(1)} %all_to_all.10.parts_ref), custom_call_target="tpu_custom_call" | custom-call | tf_op jit(solution)/shard_map/pallas_call | solution.py:147
Async XLA Ops:
  1.3 14.2 %all-to-all-start = ((bf16[8,32,128]{2,1,0:T(8,128)(2,1)}), bf16[8,32,128]{2,1,0:T(8,128)(2,1)S(1)}, u32[]{:S(2)}, u32[]{:S(2)}) async-start(bf16[8,32,128]{2,1,0:T(8,128)(2,1)} %shard_map.64), calls=%async_computation | async-start | bytes 131072 | tf_op jit(solution)/shard_map/all_to_all | solution.py:130
  15.5 1.2 %copy-start = (bf16[1024,512]{1,0:T(8,128)(2,1)S(1)}, bf16[1024,512]{1,0:T(8,128)(2,1)}, u32[]{:S(2)}) copy-start(bf16[1024,512]{1,0:T(8,128)(2,1)} %key_ref.1) | copy-start | bytes 3145732
  16.8 1.2 %copy-start.1 = (bf16[1024,512]{1,0:T(8,128)(2,1)S(1)}, bf16[1024,512]{1,0:T(8,128)(2,1)}, u32[]{:S(2)}) copy-start(bf16[1024,512]{1,0:T(8,128)(2,1)} %value_ref.1) | copy-start | bytes 3145732
  18.0 0.9 %copy-start.2 = (bf16[1,256,512]{2,1,0:T(8,128)(2,1)S(1)}, bf16[1,256,512]{2,1,0:T(8,128)(2,1)}, u32[]{:S(2)}) copy-start(bf16[1,256,512]{2,1,0:T(8,128)(2,1)} %param.9) | copy-start | bytes 786436
  18.9 0.9 %copy-start.3 = (bf16[1,256,512]{2,1,0:T(8,128)(2,1)S(1)}, bf16[1,256,512]{2,1,0:T(8,128)(2,1)}, u32[]{:S(2)}) copy-start(bf16[1,256,512]{2,1,0:T(8,128)(2,1)} %param.10) | copy-start | bytes 786436

commit v2 on v1

--- a/solution.py
+++ b/solution.py
@@ -37,27 +37,38 @@
     return lax.dot_general(a, b, (((1,), (1,)), ((), ())), preferred_element_type=jnp.float32)
 
 
-def partial_kernel(lengths_ref, query_ref, key_ref, value_ref, own_key_ref, own_value_ref, out_ref):
-    count = query_ref.shape[0]
+def own_kernel(lengths_ref, query_ref, own_key_ref, own_value_ref, key_ref, value_ref, own_ref, key_out, value_out, sems):
+    copies = [
+        pltpu.make_async_copy(key_ref, key_out, sems.at[0]),
+        pltpu.make_async_copy(value_ref, value_out, sems.at[1]),
+    ]
+    for copy in copies:
+        copy.start()
     span = own_key_ref.shape[0]
-    me = lax.axis_index("seq")
     position = lax.axis_index("grp") * span + lax.broadcasted_iota(jnp.int32, (GROUP, span), 1)
     live = position < lengths_ref[0]
-    own_query = query_ref[me].astype(jnp.float32)
-    chunks = out_ref.reshape(out_ref.shape[0] * ROWS, HEAD_DIM)
-
-    own = []
+    query = query_ref[0].astype(jnp.float32)
     for j in range(KV_HEADS):
         columns = slice(j * HEAD_DIM, (j + 1) * HEAD_DIM)
-        query = own_query[j * GROUP : (j + 1) * GROUP].astype(jnp.bfloat16)
-        scores = jnp.where(live, dot_rows(query, own_key_ref[:, columns]), LOWEST)
+        part = query[j * GROUP : (j + 1) * GROUP].astype(jnp.bfloat16)
+        scores = jnp.where(live, dot_rows(part, own_key_ref[:, columns]), LOWEST)
         peak = jnp.max(scores, axis=1, keepdims=True)
         expo = jnp.where(live, jnp.exp2((scores - peak) * LOG2_SCALE), 0.0)
         total = jnp.sum(expo, axis=1, keepdims=True)
         output = jnp.dot(
             expo.astype(jnp.bfloat16), own_value_ref[:, columns], preferred_element_type=jnp.float32
         )
-        own.append((peak, total, output))
+        own_ref[j, 0] = output
+        own_ref[j, 1] = jnp.broadcast_to(peak, (GROUP, HEAD_DIM))
+        own_ref[j, 2] = jnp.broadcast_to(total, (GROUP, HEAD_DIM))
+    for copy in copies:
+        copy.wait()
+
+
+def partial_kernel(query_ref, key_ref, value_ref, own_ref, out_ref):
+    count = query_ref.shape[0]
+    me = lax.axis_index("seq")
+    chunks = out_ref.reshape(out_ref.shape[0] * ROWS, HEAD_DIM)
 
     def one_block(block):
         queries = query_ref[pl.ds(block * BLOCK, BLOCK)].astype(jnp.float32)
@@ -76,7 +87,7 @@
             output = jnp.dot(
                 expo.astype(jnp.bfloat16), value_ref[:, columns], preferred_element_type=jnp.float32
             )
-            own_peak, own_total, own_output = own[j]
+            own_output, own_peak, own_total = own_ref[j, 0], own_ref[j, 1, :, :1], own_ref[j, 2, :, :1]
             peak = peak.reshape(BLOCK, GROUP, 1)
             total = total.reshape(BLOCK, GROUP, 1)
             output = output.reshape(BLOCK, GROUP, HEAD_DIM)
@@ -130,19 +141,30 @@
     every = lax.all_to_all(copies, "seq", 0, 0, tiled=True)
     span = suffix_keys.shape[1]
     width = KV_HEADS * HEAD_DIM
+    own, keys, values = pl.pallas_call(
+        own_kernel,
+        out_shape=(
+            pltpu.VMEM((KV_HEADS, 3, GROUP, HEAD_DIM), jnp.float32),
+            pltpu.VMEM(prompt_keys.shape, prompt_keys.dtype),
+            pltpu.VMEM(prompt_values.shape, prompt_values.dtype),
+        ),
+        in_specs=[SMEM] + [VMEM] * 3 + [pl.BlockSpec(memory_space=pl.ANY)] * 2,
+        out_specs=(VMEM, VMEM, VMEM),
+        scratch_shapes=[pltpu.SemaphoreType.DMA((2,))],
+    )(
+        lengths,
+        in_vmem(copies),
+        suffix_keys.reshape(span, width),
+        suffix_values.reshape(span, width),
+        prompt_keys,
+        prompt_values,
+    )
     partial = pl.pallas_call(
         partial_kernel,
         out_shape=pltpu.VMEM((seq * grp, 1, WIDTH), jnp.float32),
-        in_specs=[SMEM] + [VMEM] * 5,
+        in_specs=[VMEM] * 4,
         out_specs=VMEM,
-    )(
-        lengths,
-        in_vmem(every),
-        in_vmem(prompt_keys),
-        in_vmem(prompt_values),
-        in_vmem(suffix_keys.reshape(span, width)),
-        in_vmem(suffix_values.reshape(span, width)),
-    )
+    )(in_vmem(every), in_vmem(keys), in_vmem(values), in_vmem(own))
     parts = lax.all_to_all(partial, ("seq", "grp"), 0, 0, tiled=True)
     return pl.pallas_call(
         join_kernel,

time: 34 us -> 29 us (0.85)
  local copies, waits for them, and re-layouts: 4.35 us -> 0 us
  waiting for transfers between devices: 6.25 us -> 3.62 us
  Pallas kernels: 4.7 us -> 6.5 us
    unnamed x8 -> x0, local copies, waits for them, and re-layouts: 4.35 us -> none
    all_to_all x1, waiting for transfers between devices: 6.25 us -> 3.62 us  [on_device(): every = lax.all_to_all(copies, 'seq', 0, 0, tiled=True)]
    pallas_call x0 -> x1, Pallas kernels: none -> 2.63 us  [on_device(): pl.pallas_call(own_kernel, out_shape=(pltpu.VMEM((KV_HEADS, 3, GROUP, HEA...]
    pallas_call x1, Pallas kernels: 2.36 us -> 1.53 us  [on_device(): pl.pallas_call(partial_kernel, out_shape=pltpu.VMEM((seq * grp, 1, WIDTH)...]
  transfers between devices with their start and end apart: 1 -> 1, of which waited for: 1 -> 1; matrix products, arithmetic and copies ran while one was open for 0% -> 0% of each run, Pallas kernels for 0% -> 9%
where the time goes in v2:
time: 29 us; the launch traced here: 28.7 us
  blocking collectives  10.6 us (37%)
  starting transfers between devices  7.28 us (25%)
  Pallas kernels  6.5 us (22%)
  waiting for transfers between devices  3.62 us (12%)
  between operations  0.66 us (2%)
    all_to_all x1, blocking collectives, on_device(): parts = lax.all_to_all(partial, ('seq', 'grp'), 0, 0, tiled=True)  10.6 us
    all_to_all x1, starting transfers between devices, on_device(): every = lax.all_to_all(copies, 'seq', 0, 0, tiled=True)  7.28 us
    all_to_all x1, waiting for transfers between devices, on_device(): every = lax.all_to_all(copies, 'seq', 0, 0, tiled=True)  3.62 us
    pallas_call x1, Pallas kernels, on_device(): pl.pallas_call(own_kernel, out_shape=(pltpu.VMEM((KV_HEADS, 3, GROUP, HEA...  2.63 us
    pallas_call x1, Pallas kernels, on_device(): pl.pallas_call(partial_kernel, out_shape=pltpu.VMEM((seq * grp, 1, WIDTH)...  1.53 us
    pallas_call x1, Pallas kernels, on_device(): pl.pallas_call(spread_kernel, out_shape=pltpu.VMEM((seq, Q_HEADS, HEAD_DI...  1.34 us
    pallas_call x1, Pallas kernels, on_device(): pl.pallas_call(join_kernel, out_shape=jax.ShapeDtypeStruct((1, GROUP * HE...  1 us
  transfers between devices with their start and end apart: 1, of which 1 were waited for; matrix products, arithmetic and copies ran while one was open for 0% of the time, Pallas kernels for 9%

profile of v2, /device:TPU:0, one launch (start us, length us, event | category | flops | bytes accessed | tf_op | source)
XLA Modules:
  0.0 28.7 jit_solution(5880957074605966878)
XLA Ops:
  0.0 1.3 %shard_map.64.query_ref = bf16[8,32,128]{2,1,0:T(8,128)(2,1)} custom-call(bf16[1,4096]{1,0:T(2,128)(2,1)} %query_ref.1), custom_call_target="tpu_custom_call" | custom-call | tf_op jit(solution)/shard_map/pallas_call | solution.py:135
  1.3 7.3 %all-to-all-start = ((bf16[8,32,128]{2,1,0:T(8,128)(2,1)}), bf16[8,32,128]{2,1,0:T(8,128)(2,1)S(1)}, u32[]{:S(2)}, u32[]{:S(2)}) async-start(bf16[8,32,128]{2,1,0:T(8,128)(2,1)} %shard_map.64.query_ref), calls=%async_computation | async-start | bytes 131072 | tf_op jit(solution)/shard_map/all_to_all | solution.py:141
  9.3 2.6 %shard_map.65 = (f32[4,3,8,128]{3,2,1,0:T(8,128)S(1)}, bf16[1024,512]{1,0:T(8,128)(2,1)S(1)}, bf16[1024,512]{1,0:T(8,128)(2,1)S(1)}) custom-call(s32[1]{0:T(128)S(6)} %copy.7.lengths_ref, bf16[8,32,128]{2,1,0:T(8,128)(2,1)} %shard_map.64.query_ref, bf16[256,512]{1,0:T(8,128)(2,1)} %bitcast.2, bf16[256,512]{1,0:T(8,128)(2,1)} %bitcast.3, ...), custom_call_target="tpu_custom_call" | custom-call | tf_op jit(solution)/shard_map/pallas_call | solution.py:144
  11.9 3.6 %all-to-all-done.query_ref = bf16[8,32,128]{2,1,0:T(8,128)(2,1)S(1)} async-done(((bf16[8,32,128]{2,1,0:T(8,128)(2,1)}), bf16[8,32,128]{2,1,0:T(8,128)(2,1)S(1)}, u32[]{:S(2)}, u32[]{:S(2)}) %all-to-all-start) | async-done | bytes 65568 | tf_op jit(solution)/shard_map/all_to_all | solution.py:141
  15.5 1.5 %shard_map.66 = f32[32,1,1152]{2,1,0:T(1,128)S(1)} custom-call(bf16[8,32,128]{2,1,0:T(8,128)(2,1)S(1)} %all-to-all-done.query_ref, bf16[1024,512]{1,0:T(8,128)(2,1)S(1)} %get-tuple-element.8.key_ref, bf16[1024,512]{1,0:T(8,128)(2,1)S(1)} %get-tuple-element.9.value_ref, f32[4,3,8,128]{3,2,1,0:T(8,128)S(1)} %get-tuple-element.10.own_ref), custom_call_target="tpu_custom_call" | custom-call | tf_op jit(solution)/shard_map/pallas_call | solution.py:162
  17.1 10.6 %all_to_all.10.parts_ref = f32[32,1,1152]{2,1,0:T(1,128)S(1)} all-to-all(f32[32,1,1152]{2,1,0:T(1,128)S(1)} %shard_map.66), channel_id=1, replica_groups=mesh['seq'=8,'grp'=4] {'seq','grp'}, dimensions={0} | all-to-all | bytes 294912 | tf_op jit(solution)/shard_map/all_to_all | solution.py:168
  27.7 1.0 %shard_map.67 = bf16[1,1024]{1,0:T(2,128)(2,1)} custom-call(f32[32,1,1152]{2,1,0:T(1,128)S(1)} %all_to_all.10.parts_ref), custom_call_target="tpu_custom_call" | custom-call | tf_op jit(solution)/shard_map/pallas_call | solution.py:169
Async XLA Ops:
  1.3 14.2 %all-to-all-start = ((bf16[8,32,128]{2,1,0:T(8,128)(2,1)}), bf16[8,32,128]{2,1,0:T(8,128)(2,1)S(1)}, u32[]{:S(2)}, u32[]{:S(2)}) async-start(bf16[8,32,128]{2,1,0:T(8,128)(2,1)} %shard_map.64.query_ref), calls=%async_computation | async-start | bytes 131072 | tf_op jit(solution)/shard_map/all_to_all | solution.py:141

commit v3 on v2

v3 whole, which is shorter than its diff:
```python
import functools
import math

import jax
import jax.numpy as jnp
from jax import lax
from jax.experimental import pallas as pl
from jax.experimental.pallas import tpu as pltpu
from jax.sharding import PartitionSpec as P

Q_HEADS = 32
KV_HEADS = 4
HEAD_DIM = 128
GROUP = 8
PAIRS = KV_HEADS // 2
PAIR_DIM = 2 * HEAD_DIM
BLOCK = 8
BLOCK_ROWS = BLOCK * GROUP
ROWS = GROUP + 1
WIDTH = ROWS * HEAD_DIM
SCALE = 1.0 / math.sqrt(HEAD_DIM)
LOWEST = -1e30

VMEM = pl.BlockSpec(memory_space=pltpu.VMEM)
ANY = pl.BlockSpec(memory_space=pl.ANY)


def in_vmem(x):
    return pltpu.with_memory_space_constraint(x, pltpu.VMEM)


def spread_kernel(query_ref, key_ref, out_ref, key_out, query, copies, sems):
    query_in = pltpu.make_async_copy(query_ref, query, sems.at[0])
    keys_in = pltpu.make_async_copy(key_ref, key_out, sems.at[1])
    copies_out = pltpu.make_async_copy(copies, out_ref, sems.at[2])
    query_in.start()
    keys_in.start()
    query_in.wait()
    row = query[...].astype(jnp.float32)
    rows = [row[:, h * HEAD_DIM : (h + 1) * HEAD_DIM] for h in range(Q_HEADS)]
    rows = jnp.concatenate(rows, axis=0).astype(copies.dtype)
    copies[...] = jnp.broadcast_to(rows[None], copies.shape)
    copies_out.start()
    copies_out.wait()
    keys_in.wait()


def dot_rows(a, b):
    return lax.dot_general(a, b, (((1,), (1,)), ((), ())), preferred_element_type=jnp.float32)


def side_by_side(first, second):
    zero = jnp.zeros_like(first)
    rows = [jnp.concatenate([first, zero], axis=1), jnp.concatenate([zero, second], axis=1)]
    return jnp.concatenate(rows, axis=0).astype(jnp.bfloat16)


def in_lanes(columns, rows):
    lane = lax.broadcasted_iota(jnp.int32, (rows, HEAD_DIM), 1)
    out = jnp.zeros((rows, HEAD_DIM), jnp.float32)
    for j, column in enumerate(columns):
        out = jnp.where(lane == j, column, out)
    return out


def own_kernel(
    lengths_ref, copies_ref, own_key_ref, own_value_ref, value_ref,
    own_ref, sums_ref, value_out,
    length, query_buf, own_key, own_value, sems,
):
    moves = (
        (copies_ref.at[0], query_buf),
        (own_key_ref, own_key),
        (lengths_ref, length),
        (own_value_ref, own_value),
        (value_ref, value_out),
    )
    moves = [pltpu.make_async_copy(a, b, sems.at[i]) for i, (a, b) in enumerate(moves)]
    for move in moves:
        move.start()
    span = own_key.shape[0]
    position = lax.broadcasted_iota(jnp.int32, (2 * GROUP, span), 1) + lax.axis_index("grp") * span
    moves[0].wait()
    query = query_buf[...].astype(jnp.float32)
    moves[1].wait()
    scores = []
    for i in range(PAIRS):
        top = 2 * i * GROUP
        both = side_by_side(query[top : top + GROUP], query[top + GROUP : top + 2 * GROUP])
        scores.append(dot_rows(both, own_key[:, i * PAIR_DIM : (i + 1) * PAIR_DIM]))
    moves[2].wait()
    live = position < length[...]
    moves[3].wait()
    peaks, totals = [], []
    for i in range(PAIRS):
        masked = jnp.where(live, scores[i], LOWEST)
        peak = jnp.max(masked, axis=1, keepdims=True)
        expo = jnp.where(live, jnp.exp((masked - peak) * SCALE), 0.0)
        total = jnp.sum(expo, axis=1, keepdims=True)
        output = jnp.dot(
            expo.astype(jnp.bfloat16),
            own_value[:, i * PAIR_DIM : (i + 1) * PAIR_DIM],
            preferred_element_type=jnp.float32,
        )
        own_ref[2 * i] = output[:GROUP, :HEAD_DIM]
        own_ref[2 * i + 1] = output[GROUP:, HEAD_DIM:]
        peaks += [peak[:GROUP], peak[GROUP:]]
        totals += [total[:GROUP], total[GROUP:]]
    sums_ref[0] = in_lanes(peaks, GROUP)
    sums_ref[1] = in_lanes(totals, GROUP)
    moves[4].wait()


def partial_kernel(query_ref, key_ref, value_ref, own_ref, own_sums_ref, out_ref, sums_ref):
    count = query_ref.shape[0]
    me = lax.axis_index("seq")
    chunks = out_ref.reshape(out_ref.shape[0] * ROWS, HEAD_DIM)

    def join_own():
        row = (me % BLOCK) * GROUP
        peak, total = sums_ref[pl.ds(row, GROUP)], sums_ref[pl.ds(BLOCK_ROWS + row, GROUP)]
        own_peak, own_total = own_sums_ref[0], own_sums_ref[1]
        joined = jnp.maximum(peak, own_peak)
        factor = jnp.exp((peak - joined) * SCALE)
        own_factor = jnp.exp((own_peak - joined) * SCALE)
        sums_ref[pl.ds(row, GROUP)] = joined
        sums_ref[pl.ds(BLOCK_ROWS + row, GROUP)] = total * factor + own_total * own_factor
        for j in range(KV_HEADS):
            rows = pl.ds((me * KV_HEADS + j) * ROWS, GROUP)
            chunks[rows] = chunks[rows] * factor[:, j : j + 1] + own_ref[j] * own_factor[:, j : j + 1]

    def one_block(block):
        queries = query_ref[pl.ds(block * BLOCK, BLOCK)].astype(jnp.float32)
        heads = [
            queries[:, j * GROUP : (j + 1) * GROUP].reshape(BLOCK_ROWS, HEAD_DIM)
            for j in range(KV_HEADS)
        ]
        scores = [
            dot_rows(
                side_by_side(heads[2 * i], heads[2 * i + 1]),
                key_ref[:, i * PAIR_DIM : (i + 1) * PAIR_DIM],
            )
            for i in range(PAIRS)
        ]
        peaks, totals = [], []
        for i in range(PAIRS):
            peak = jnp.max(scores[i], axis=1, keepdims=True)
            expo = jnp.exp((scores[i] - peak) * SCALE)
            total = jnp.sum(expo, axis=1, keepdims=True)
            output = jnp.dot(
                expo.astype(jnp.bfloat16),
                value_ref[:, i * PAIR_DIM : (i + 1) * PAIR_DIM],
                preferred_element_type=jnp.float32,
            )
            for r in range(BLOCK):
                for h in range(2):
                    rows = slice(h * BLOCK_ROWS + r * GROUP, h * BLOCK_ROWS + (r + 1) * GROUP)
                    chunk = ((block * BLOCK + r) * KV_HEADS + 2 * i + h) * ROWS
                    chunks[pl.ds(chunk, GROUP)] = output[rows, h * HEAD_DIM : (h + 1) * HEAD_DIM]
            peaks += [peak[:BLOCK_ROWS], peak[BLOCK_ROWS:]]
            totals += [total[:BLOCK_ROWS], total[BLOCK_ROWS:]]
        sums_ref[:BLOCK_ROWS] = in_lanes(peaks, BLOCK_ROWS)
        sums_ref[BLOCK_ROWS:] = in_lanes(totals, BLOCK_ROWS)
        if count == BLOCK:
            join_own()
        else:
            pl.when(me // BLOCK == block)(join_own)
        sums = sums_ref[...].T
        for r in range(BLOCK):
            for j in range(KV_HEADS):
                chunk = ((block * BLOCK + r) * KV_HEADS + j) * ROWS
                chunks[pl.ds(chunk + GROUP, 1)] = sums[j : j + 1]

    if count == BLOCK:
        one_block(0)
    else:
        pl.loop(0, count // BLOCK)(one_block)


def join_kernel(parts_ref, out_ref):
    sums = parts_ref[:, 0, GROUP * HEAD_DIM :]
    offset = (lax.axis_index("seq") % BLOCK) * GROUP
    peaks = pltpu.roll(sums, (HEAD_DIM - offset) % HEAD_DIM, 1)
    totals = pltpu.roll(peaks, HEAD_DIM - BLOCK_ROWS, 1)
    factor = jnp.exp((peaks - jnp.max(peaks, axis=0, keepdims=True)) * SCALE)
    factor = factor / jnp.sum(factor * totals, axis=0, keepdims=True)
    for h in range(GROUP):
        columns = slice(h * HEAD_DIM, (h + 1) * HEAD_DIM)
        output = jnp.sum(parts_ref[:, 0, columns] * factor[:, h : h + 1], axis=0, keepdims=True)
        out_ref[:, columns] = output.astype(out_ref.dtype)


def on_device(seq, grp, queries, prompt_keys, prompt_values, suffix_keys, suffix_values, lengths):
    copies, keys = pl.pallas_call(
        spread_kernel,
        out_shape=(
            jax.ShapeDtypeStruct((seq, Q_HEADS, HEAD_DIM), queries.dtype),
            pltpu.VMEM(prompt_keys.shape, prompt_keys.dtype),
        ),
        in_specs=[ANY] * 2,
        out_specs=(ANY, VMEM),
        scratch_shapes=[
            pltpu.VMEM(queries.shape, queries.dtype),
            pltpu.VMEM((seq, Q_HEADS, HEAD_DIM), queries.dtype),
            pltpu.SemaphoreType.DMA((3,)),
        ],
    )(queries, prompt_keys)
    every = lax.all_to_all(copies, "seq", 0, 0, tiled=True)
    span = suffix_keys.shape[1]
    width = KV_HEADS * HEAD_DIM
    own, own_sums, values = pl.pallas_call(
        own_kernel,
        out_shape=(
            pltpu.VMEM((KV_HEADS, GROUP, HEAD_DIM), jnp.float32),
            pltpu.VMEM((2, GROUP, HEAD_DIM), jnp.float32),
            pltpu.VMEM(prompt_values.shape, prompt_values.dtype),
        ),
        in_specs=[ANY] * 5,
        out_specs=(VMEM,) * 3,
        scratch_shapes=[
            pltpu.VMEM((1, 1), jnp.int32),
            pltpu.VMEM((Q_HEADS, HEAD_DIM), queries.dtype),
            pltpu.VMEM((span, width), suffix_keys.dtype),
            pltpu.VMEM((span, width), suffix_values.dtype),
            pltpu.SemaphoreType.DMA((5,)),
        ],
    )(
        lengths.reshape(1, 1),
        copies,
        suffix_keys.reshape(span, width),
        suffix_values.reshape(span, width),
        prompt_values,
    )
    partial = pl.pallas_call(
        partial_kernel,
        out_shape=pltpu.VMEM((seq * grp, 1, WIDTH), jnp.float32),
        in_specs=[VMEM] * 5,
        out_specs=VMEM,
        scratch_shapes=[pltpu.VMEM((2 * BLOCK_ROWS, HEAD_DIM), jnp.float32)],
    )(in_vmem(every), in_vmem(keys), in_vmem(values), in_vmem(own), in_vmem(own_sums))
    parts = lax.all_to_all(partial, ("seq", "grp"), 0, 0, tiled=True)
    return pl.pallas_call(
        join_kernel,
        out_shape=jax.ShapeDtypeStruct((1, GROUP * HEAD_DIM), queries.dtype),
        in_specs=[VMEM],
        out_specs=VMEM,
    )(in_vmem(parts))


def solution(mesh):
    in_specs = (
        P("seq", None),
        P(("seq", "grp"), None),
        P(("seq", "grp"), None),
        P("seq", "grp", None),
        P("seq", "grp", None),
        P("seq"),
    )
    return jax.shard_map(
        functools.partial(on_device, mesh.shape["seq"], mesh.shape["grp"]),
        mesh=mesh,
        in_specs=in_specs,
        out_specs=P("seq", "grp"),
        check_vma=False,
    )
```

time: 29 us -> 28.2 us (0.972)
  Pallas kernels: 6.5 us -> 4.66 us
  waiting for transfers between devices: 3.62 us -> 4.77 us
  blocking collectives: 10.6 us -> 10.3 us
    all_to_all x1, waiting for transfers between devices: 3.62 us -> 4.77 us  [on_device(): every = lax.all_to_all(copies, 'seq', 0, 0, tiled=True)]
    pallas_call x2, Pallas kernels: 3.97 us -> 2.85 us  [the longest x1 1.48 us: on_device(): pl.pallas_call(own_kernel, out_shape=(pltpu.VMEM((KV_HEADS, GROUP, HEAD_D...]
    pallas_call x1, Pallas kernels: 1.53 us -> 0.93 us  [on_device(): pl.pallas_call(partial_kernel, out_shape=pltpu.VMEM((seq * grp, 1, WIDTH)...]
    all_to_all x1, blocking collectives: 10.6 us -> 10.3 us  [on_device(): parts = lax.all_to_all(partial, ('seq', 'grp'), 0, 0, tiled=True)]
  transfers between devices with their start and end apart: 1 -> 1, of which waited for: 1 -> 1; matrix products, arithmetic and copies ran while one was open for 0% -> 0% of each run, Pallas kernels for 9% -> 5%
where the time goes in v3:
time: 28.2 us; the launch traced here: 27.7 us
  blocking collectives  10.3 us (37%)
  starting transfers between devices  7.29 us (26%)
  waiting for transfers between devices  4.77 us (17%)
  Pallas kernels  4.66 us (17%)
  between operations  0.67 us (2%)
    all_to_all x1, blocking collectives, on_device(): parts = lax.all_to_all(partial, ('seq', 'grp'), 0, 0, tiled=True)  10.3 us
    all_to_all x1, starting transfers between devices, on_device(): every = lax.all_to_all(copies, 'seq', 0, 0, tiled=True)  7.29 us
    all_to_all x1, waiting for transfers between devices, on_device(): every = lax.all_to_all(copies, 'seq', 0, 0, tiled=True)  4.77 us
    pallas_call x1, Pallas kernels, on_device(): pl.pallas_call(own_kernel, out_shape=(pltpu.VMEM((KV_HEADS, GROUP, HEAD_D...  1.48 us
    pallas_call x1, Pallas kernels, on_device(): pl.pallas_call(spread_kernel, out_shape=(jax.ShapeDtypeStruct((seq, Q_HEA...  1.37 us
    pallas_call x1, Pallas kernels, on_device(): pl.pallas_call(partial_kernel, out_shape=pltpu.VMEM((seq * grp, 1, WIDTH)...  0.93 us
    pallas_call x1, Pallas kernels, on_device(): pl.pallas_call(join_kernel, out_shape=jax.ShapeDtypeStruct((1, GROUP * HE...  0.89 us
  transfers between devices with their start and end apart: 1, of which 1 were waited for; matrix products, arithmetic and copies ran while one was open for 0% of the time, Pallas kernels for 5%

profile of v3, /device:TPU:0, one launch (start us, length us, event | category | flops | bytes accessed | tf_op | source)
XLA Modules:
  0.0 27.7 jit_solution(9470294380075317125)
XLA Ops:
  0.0 1.4 %shard_map.64 = (bf16[8,32,128]{2,1,0:T(8,128)(2,1)}, bf16[1024,512]{1,0:T(8,128)(2,1)S(1)}) custom-call(bf16[1,4096]{1,0:T(2,128)(2,1)} %query_ref.1, bf16[1024,512]{1,0:T(8,128)(2,1)} %key_ref.1), custom_call_target="tpu_custom_call" | custom-call | tf_op jit(solution)/shard_map/pallas_call | solution.py:194
  1.4 7.3 %all-to-all-start = ((bf16[8,32,128]{2,1,0:T(8,128)(2,1)}), bf16[8,32,128]{2,1,0:T(8,128)(2,1)S(1)}, u32[]{:S(2)}, u32[]{:S(2)}) async-start(bf16[8,32,128]{2,1,0:T(8,128)(2,1)} %get-tuple-element.10.copies_ref), calls=%async_computation | async-start | bytes 131072 | tf_op jit(solution)/shard_map/all_to_all | solution.py:208
  9.3 1.5 %shard_map.65 = (f32[4,8,128]{2,1,0:T(8,128)S(1)}, f32[2,8,128]{2,1,0:T(8,128)S(1)}, bf16[1024,512]{1,0:T(8,128)(2,1)S(1)}) custom-call(s32[1,1]{1,0:T(1,128)} %bitcast.3.lengths_ref, bf16[8,32,128]{2,1,0:T(8,128)(2,1)} %get-tuple-element.10.copies_ref, bf16[256,512]{1,0:T(8,128)(2,1)} %bitcast.4, bf16[256,512]{1,0:T(8,128)(2,1)} %bitcast.5, ...), custom_call_target="tpu_custom_call" | custom-call | tf_op jit(solution)/shard_map/pallas_call | solution.py:211
  10.8 4.8 %all-to-all-done.query_ref = bf16[8,32,128]{2,1,0:T(8,128)(2,1)S(1)} async-done(((bf16[8,32,128]{2,1,0:T(8,128)(2,1)}), bf16[8,32,128]{2,1,0:T(8,128)(2,1)S(1)}, u32[]{:S(2)}, u32[]{:S(2)}) %all-to-all-start) | async-done | bytes 65568 | tf_op jit(solution)/shard_map/all_to_all | solution.py:208
  15.6 0.9 %shard_map.66 = f32[32,1,1152]{2,1,0:T(1,128)S(1)} custom-call(bf16[8,32,128]{2,1,0:T(8,128)(2,1)S(1)} %all-to-all-done.query_ref, bf16[1024,512]{1,0:T(8,128)(2,1)S(1)} %get-tuple-element.11.key_ref, bf16[1024,512]{1,0:T(8,128)(2,1)S(1)} %get-tuple-element.12.value_ref, f32[4,8,128]{2,1,0:T(8,128)S(1)} %get-tuple-element.13.own_ref, ...), custom_call_target="tpu_custom_call" | custom-call | tf_op jit(solution)/shard_map/pallas_call | solution.py:234
  16.5 10.3 %all_to_all.10.parts_ref = f32[32,1,1152]{2,1,0:T(1,128)S(1)} all-to-all(f32[32,1,1152]{2,1,0:T(1,128)S(1)} %shard_map.66), channel_id=1, replica_groups=mesh['seq'=8,'grp'=4] {'seq','grp'}, dimensions={0} | all-to-all | bytes 294912 | tf_op jit(solution)/shard_map/all_to_all | solution.py:241
  26.8 0.9 %shard_map.67 = bf16[1,1024]{1,0:T(2,128)(2,1)} custom-call(f32[32,1,1152]{2,1,0:T(1,128)S(1)} %all_to_all.10.parts_ref), custom_call_target="tpu_custom_call" | custom-call | tf_op jit(solution)/shard_map/pallas_call | solution.py:242
Async XLA Ops:
  1.4 14.2 %all-to-all-start = ((bf16[8,32,128]{2,1,0:T(8,128)(2,1)}), bf16[8,32,128]{2,1,0:T(8,128)(2,1)S(1)}, u32[]{:S(2)}, u32[]{:S(2)}) async-start(bf16[8,32,128]{2,1,0:T(8,128)(2,1)} %get-tuple-element.10.copies_ref), calls=%async_computation | async-start | bytes 131072 | tf_op jit(solution)/shard_map/all_to_all | solution.py:208

commit v4 on v3

--- a/solution.py
+++ b/solution.py
@@ -16,10 +16,13 @@
 PAIR_DIM = 2 * HEAD_DIM
 BLOCK = 8
 BLOCK_ROWS = BLOCK * GROUP
-ROWS = GROUP + 1
-WIDTH = ROWS * HEAD_DIM
+ROWS = GROUP + 2
+SHARED = 2
+DIRECT = ((5, 7), (3, 4), (1, 6))
+COARSE = 8.0
 SCALE = 1.0 / math.sqrt(HEAD_DIM)
 LOWEST = -1e30
+SMALLEST = 2.0**-120
 
 VMEM = pl.BlockSpec(memory_space=pltpu.VMEM)
 ANY = pl.BlockSpec(memory_space=pl.ANY)
@@ -29,20 +32,22 @@
     return pltpu.with_memory_space_constraint(x, pltpu.VMEM)
 
 
-def spread_kernel(query_ref, key_ref, out_ref, key_out, query, copies, sems):
-    query_in = pltpu.make_async_copy(query_ref, query, sems.at[0])
-    keys_in = pltpu.make_async_copy(key_ref, key_out, sems.at[1])
-    copies_out = pltpu.make_async_copy(copies, out_ref, sems.at[2])
-    query_in.start()
-    keys_in.start()
-    query_in.wait()
-    row = query[...].astype(jnp.float32)
+def head_rows(query_ref):
+    row = query_ref[...].astype(jnp.float32)
     rows = [row[:, h * HEAD_DIM : (h + 1) * HEAD_DIM] for h in range(Q_HEADS)]
-    rows = jnp.concatenate(rows, axis=0).astype(copies.dtype)
-    copies[...] = jnp.broadcast_to(rows[None], copies.shape)
-    copies_out.start()
-    copies_out.wait()
-    keys_in.wait()
+    return jnp.concatenate(rows, axis=0).astype(query_ref.dtype)
+
+
+def spread_kernel(query_ref, out_ref):
+    out_ref[...] = jnp.broadcast_to(head_rows(query_ref)[None], out_ref.shape)
+
+
+def collect_kernel(own_ref, shared_ref, *refs):
+    *direct_refs, near_ref, mine_ref = refs
+    near_ref[0] = own_ref[...]
+    near_ref[1] = head_rows(shared_ref)
+    for i, ref in enumerate(direct_refs):
+        mine_ref[i] = head_rows(ref)
 
 
 def dot_rows(a, b):
@@ -64,16 +69,17 @@
 
 
 def own_kernel(
-    lengths_ref, copies_ref, own_key_ref, own_value_ref, value_ref,
-    own_ref, sums_ref, value_out,
+    lengths_ref, query_ref, own_key_ref, own_value_ref, key_ref, value_ref,
+    own_ref, sums_ref, rows_ref, key_out, value_out,
     length, query_buf, own_key, own_value, sems,
 ):
     moves = (
-        (copies_ref.at[0], query_buf),
+        (query_ref, query_buf),
         (own_key_ref, own_key),
         (lengths_ref, length),
         (own_value_ref, own_value),
         (value_ref, value_out),
+        (key_ref, key_out),
     )
     moves = [pltpu.make_async_copy(a, b, sems.at[i]) for i, (a, b) in enumerate(moves)]
     for move in moves:
@@ -81,7 +87,8 @@
     span = own_key.shape[0]
     position = lax.broadcasted_iota(jnp.int32, (2 * GROUP, span), 1) + lax.axis_index("grp") * span
     moves[0].wait()
-    query = query_buf[...].astype(jnp.float32)
+    rows_ref[...] = head_rows(query_buf)
+    query = rows_ref[...].astype(jnp.float32)
     moves[1].wait()
     scores = []
     for i in range(PAIRS):
@@ -106,15 +113,41 @@
         own_ref[2 * i + 1] = output[GROUP:, HEAD_DIM:]
         peaks += [peak[:GROUP], peak[GROUP:]]
         totals += [total[:GROUP], total[GROUP:]]
+    largest = jnp.max(jnp.abs(own_value[...]), axis=0, keepdims=True)
+    moves[4].wait()
+    largest = jnp.maximum(largest, jnp.max(jnp.abs(value_out[...]), axis=0, keepdims=True))
+    largest = jnp.max(largest.astype(jnp.float32), axis=1, keepdims=True)
+    power = jnp.ceil(jnp.log2(jnp.maximum(largest, SMALLEST)))
+    power -= 15 - (key_ref.shape[0] + span - 1).bit_length()
+    shrink = jnp.exp2(-power)
+    for j in range(KV_HEADS):
+        own_ref[j] *= shrink
     sums_ref[0] = in_lanes(peaks, GROUP)
     sums_ref[1] = in_lanes(totals, GROUP)
-    moves[4].wait()
-
-
-def partial_kernel(query_ref, key_ref, value_ref, own_ref, own_sums_ref, out_ref, sums_ref):
+    sums_ref[2] = jnp.broadcast_to(power * (math.log(2.0) / SCALE), (GROUP, HEAD_DIM))
+    sums_ref[3] = jnp.broadcast_to(shrink, (GROUP, HEAD_DIM))
+    moves[5].wait()
+
+
+def partial_kernel(
+    gathered, key_ref, value_ref, own_ref, own_sums_ref, *refs
+):
+    me = lax.axis_index("seq")
+    if gathered:
+        query_ref, out_ref, sums_ref = refs
+    else:
+        near_ref, mine_ref, other_ref, out_ref, sums_ref, query_ref = refs
+        core = lax.axis_index("grp") % 2
+        query_ref[me] = near_ref[0]
+        query_ref[me ^ SHARED] = near_ref[1]
+        for i, (even, odd) in enumerate(DIRECT):
+            query_ref[me ^ jnp.where(core == 0, even, odd)] = mine_ref[i]
+            query_ref[me ^ jnp.where(core == 0, odd, even)] = other_ref[i]
     count = query_ref.shape[0]
-    me = lax.axis_index("seq")
-    chunks = out_ref.reshape(out_ref.shape[0] * ROWS, HEAD_DIM)
+    shrink = own_sums_ref[3, :1, :1]
+
+    def columns(i):
+        return slice(i * HEAD_DIM, (i + 1) * HEAD_DIM)
 
     def join_own():
         row = (me % BLOCK) * GROUP
@@ -127,7 +160,7 @@
         sums_ref[pl.ds(BLOCK_ROWS + row, GROUP)] = total * factor + own_total * own_factor
         for j in range(KV_HEADS):
             rows = pl.ds((me * KV_HEADS + j) * ROWS, GROUP)
-            chunks[rows] = chunks[rows] * factor[:, j : j + 1] + own_ref[j] * own_factor[:, j : j + 1]
+            out_ref[rows] = out_ref[rows] * factor[:, j : j + 1] + own_ref[j] * own_factor[:, j : j + 1]
 
     def one_block(block):
         queries = query_ref[pl.ds(block * BLOCK, BLOCK)].astype(jnp.float32)
@@ -156,7 +189,7 @@
                 for h in range(2):
                     rows = slice(h * BLOCK_ROWS + r * GROUP, h * BLOCK_ROWS + (r + 1) * GROUP)
                     chunk = ((block * BLOCK + r) * KV_HEADS + 2 * i + h) * ROWS
-                    chunks[pl.ds(chunk, GROUP)] = output[rows, h * HEAD_DIM : (h + 1) * HEAD_DIM]
+                    out_ref[pl.ds(chunk, GROUP)] = output[rows, columns(h)] * shrink
             peaks += [peak[:BLOCK_ROWS], peak[BLOCK_ROWS:]]
             totals += [total[:BLOCK_ROWS], total[BLOCK_ROWS:]]
         sums_ref[:BLOCK_ROWS] = in_lanes(peaks, BLOCK_ROWS)
@@ -165,11 +198,19 @@
             join_own()
         else:
             pl.when(me // BLOCK == block)(join_own)
-        sums = sums_ref[...].T
+        sums = sums_ref[...].T[:GROUP]
+        lane = lax.broadcasted_iota(jnp.int32, (GROUP, HEAD_DIM), 1)
+        peaks = jnp.where(lane < BLOCK_ROWS, sums, pltpu.roll(sums, BLOCK_ROWS, 1))
+        weights = peaks + jnp.where(
+            lane < BLOCK_ROWS, own_sums_ref[2], jnp.log(sums) * (1.0 / SCALE)
+        )
+        coarse = jnp.round(weights * (1.0 / COARSE)) * COARSE
+        fine = weights - coarse
         for r in range(BLOCK):
             for j in range(KV_HEADS):
                 chunk = ((block * BLOCK + r) * KV_HEADS + j) * ROWS
-                chunks[pl.ds(chunk + GROUP, 1)] = sums[j : j + 1]
+                out_ref[pl.ds(chunk + GROUP, 1)] = coarse[j : j + 1]
+                out_ref[pl.ds(chunk + GROUP + 1, 1)] = fine[j : j + 1]
 
     if count == BLOCK:
         one_block(0)
@@ -178,67 +219,93 @@
 
 
 def join_kernel(parts_ref, out_ref):
-    sums = parts_ref[:, 0, GROUP * HEAD_DIM :]
+    parts = parts_ref.shape[0] // ROWS
+
+    def every(row):
+        return parts_ref[pl.ds(row, parts, stride=ROWS)]
+
     offset = (lax.axis_index("seq") % BLOCK) * GROUP
-    peaks = pltpu.roll(sums, (HEAD_DIM - offset) % HEAD_DIM, 1)
-    totals = pltpu.roll(peaks, HEAD_DIM - BLOCK_ROWS, 1)
-    factor = jnp.exp((peaks - jnp.max(peaks, axis=0, keepdims=True)) * SCALE)
-    factor = factor / jnp.sum(factor * totals, axis=0, keepdims=True)
+    weights = pltpu.roll(every(GROUP) + every(GROUP + 1), (HEAD_DIM - offset) % HEAD_DIM, 1)
+    totals = pltpu.roll(weights, HEAD_DIM - BLOCK_ROWS, 1)
+    top = jnp.max(totals, axis=0, keepdims=True)
+    total = jnp.sum(jnp.exp((totals - top) * SCALE), axis=0, keepdims=True)
+    factor = jnp.exp((weights - top) * SCALE) / total
     for h in range(GROUP):
-        columns = slice(h * HEAD_DIM, (h + 1) * HEAD_DIM)
-        output = jnp.sum(parts_ref[:, 0, columns] * factor[:, h : h + 1], axis=0, keepdims=True)
-        out_ref[:, columns] = output.astype(out_ref.dtype)
+        output = jnp.sum(every(h) * factor[:, h : h + 1], axis=0, keepdims=True)
+        out_ref[:, h * HEAD_DIM : (h + 1) * HEAD_DIM] = output.astype(out_ref.dtype)
+
+
+def straight(seq, grp, even, odd):
+    return [
+        (i * grp + j, (i ^ (odd if j % 2 else even)) * grp + j) for i in range(seq) for j in range(grp)
+    ]
 
 
 def on_device(seq, grp, queries, prompt_keys, prompt_values, suffix_keys, suffix_values, lengths):
-    copies, keys = pl.pallas_call(
-        spread_kernel,
-        out_shape=(
-            jax.ShapeDtypeStruct((seq, Q_HEADS, HEAD_DIM), queries.dtype),
-            pltpu.VMEM(prompt_keys.shape, prompt_keys.dtype),
-        ),
-        in_specs=[ANY] * 2,
-        out_specs=(ANY, VMEM),
-        scratch_shapes=[
-            pltpu.VMEM(queries.shape, queries.dtype),
-            pltpu.VMEM((seq, Q_HEADS, HEAD_DIM), queries.dtype),
-            pltpu.SemaphoreType.DMA((3,)),
-        ],
-    )(queries, prompt_keys)
-    every = lax.all_to_all(copies, "seq", 0, 0, tiled=True)
     span = suffix_keys.shape[1]
     width = KV_HEADS * HEAD_DIM
-    own, own_sums, values = pl.pallas_call(
+    own, own_sums, rows, keys, values = pl.pallas_call(
         own_kernel,
         out_shape=(
             pltpu.VMEM((KV_HEADS, GROUP, HEAD_DIM), jnp.float32),
-            pltpu.VMEM((2, GROUP, HEAD_DIM), jnp.float32),
+            pltpu.VMEM((4, GROUP, HEAD_DIM), jnp.float32),
+            pltpu.VMEM((Q_HEADS, HEAD_DIM), queries.dtype),
+            pltpu.VMEM(prompt_keys.shape, prompt_keys.dtype),
             pltpu.VMEM(prompt_values.shape, prompt_values.dtype),
         ),
-        in_specs=[ANY] * 5,
-        out_specs=(VMEM,) * 3,
+        in_specs=[ANY] * 6,
+        out_specs=(VMEM,) * 5,
         scratch_shapes=[
             pltpu.VMEM((1, 1), jnp.int32),
-            pltpu.VMEM((Q_HEADS, HEAD_DIM), queries.dtype),
+            pltpu.VMEM(queries.shape, queries.dtype),
             pltpu.VMEM((span, width), suffix_keys.dtype),
             pltpu.VMEM((span, width), suffix_values.dtype),
-            pltpu.SemaphoreType.DMA((5,)),
+            pltpu.SemaphoreType.DMA((6,)),
         ],
     )(
         lengths.reshape(1, 1),
-        copies,
+        queries,
         suffix_keys.reshape(span, width),
         suffix_values.reshape(span, width),
+        prompt_keys,
         prompt_values,
     )
+    scratch = [pltpu.VMEM((2 * BLOCK_ROWS, HEAD_DIM), jnp.float32)]
+    if seq == BLOCK and grp % 2 == 0:
+        direct = [
+            lax.ppermute(queries, ("seq", "grp"), straight(seq, grp, even, odd)) for even, odd in DIRECT
+        ]
+        shared = lax.ppermute(queries, ("seq", "grp"), straight(seq, grp, SHARED, SHARED))
+        near, mine = pl.pallas_call(
+            collect_kernel,
+            out_shape=(
+                pltpu.VMEM((2, Q_HEADS, HEAD_DIM), queries.dtype),
+                pltpu.VMEM((len(DIRECT), Q_HEADS, HEAD_DIM), queries.dtype),
+            ),
+            in_specs=[VMEM] * (2 + len(DIRECT)),
+            out_specs=(VMEM, VMEM),
+        )(in_vmem(rows), in_vmem(shared), *map(in_vmem, direct))
+        other = lax.ppermute(mine, "grp", [(j, j ^ 1) for j in range(grp)])
+        every = [near, mine, other]
+        scratch.append(pltpu.VMEM((seq, Q_HEADS, HEAD_DIM), queries.dtype))
+    else:
+        copies = pl.pallas_call(
+            spread_kernel,
+            out_shape=pltpu.VMEM((seq, Q_HEADS, HEAD_DIM), queries.dtype),
+            in_specs=[VMEM],
+            out_specs=VMEM,
+        )(queries)
+        every = [lax.all_to_all(copies, "seq", 0, 0, tiled=True)]
     partial = pl.pallas_call(
-        partial_kernel,
-        out_shape=pltpu.VMEM((seq * grp, 1, WIDTH), jnp.float32),
-        in_specs=[VMEM] * 5,
+        functools.partial(partial_kernel, len(every) == 1),
+        out_shape=pltpu.VMEM((seq * grp * ROWS, HEAD_DIM), jnp.float32),
+        in_specs=[VMEM] * (4 + len(every)),
         out_specs=VMEM,
-        scratch_shapes=[pltpu.VMEM((2 * BLOCK_ROWS, HEAD_DIM), jnp.float32)],
-    )(in_vmem(every), in_vmem(keys), in_vmem(values), in_vmem(own), in_vmem(own_sums))
+        scratch_shapes=scratch,
+    )(in_vmem(keys), in_vmem(values), in_vmem(own), in_vmem(own_sums), *map(in_vmem, every))
+    partial = partial.reshape(seq * grp, ROWS // 2, 2, HEAD_DIM).astype(jnp.float16)
     parts = lax.all_to_all(partial, ("seq", "grp"), 0, 0, tiled=True)
+    parts = parts.astype(jnp.float32).reshape(seq * grp * ROWS, HEAD_DIM)
     return pl.pallas_call(
         join_kernel,
         out_shape=jax.ShapeDtypeStruct((1, GROUP * HEAD_DIM), queries.dtype),

time: 28.2 us -> 25.7 us (0.911)
  waiting for transfers between devices: 4.77 us -> 2.17 us
  starting transfers between devices: 7.29 us -> 8.55 us
  Pallas kernels: 4.66 us -> 3.71 us
    ppermute x0 -> x5, starting transfers between devices: none -> 8.55 us  [the longest x3 6.9 us: on_device(): lax.ppermute(queries, ('seq', 'grp'), straight(seq, grp, even, odd))]
    all_to_all x1 -> x0, starting transfers between devices: 7.29 us -> none  [on_device(): every = lax.all_to_all(copies, 'seq', 0, 0, tiled=True)]
    all_to_all x1 -> x0, waiting for transfers between devices: 4.77 us -> none  [on_device(): every = lax.all_to_all(copies, 'seq', 0, 0, tiled=True)]
    ppermute x0 -> x5, waiting for transfers between devices: none -> 2.17 us  [the longest x1 1.18 us: on_device(): other = lax.ppermute(mine, 'grp', [(j, j ^ 1) for j in range(grp)])]
    pallas_call x2, Pallas kernels: 2.3 us -> 1.02 us  [the longest x1 0.98 us: on_device(): pl.pallas_call(functools.partial(partial_kernel, len(every) == 1), out_sh...]
    pallas_call x1, Pallas kernels: 1.48 us -> 1.78 us  [on_device(): pl.pallas_call(own_kernel, out_shape=(pltpu.VMEM((KV_HEADS, GROUP, HEAD_D...]
  transfers between devices with their start and end apart: 1 -> 5, of which waited for: 1 -> 2; matrix products, arithmetic and copies ran while one was open for 0% -> 0% of each run, Pallas kernels for 5% -> 7%
where the time goes in v4:
time: 25.7 us; the launch traced here: 25.4 us
  blocking collectives  10.2 us (40%)
  starting transfers between devices  8.55 us (33%)
  Pallas kernels  3.71 us (14%)
  waiting for transfers between devices  2.17 us (8%)
  between operations  0.72 us (3%)
    all_to_all x1, blocking collectives, on_device(): parts = lax.all_to_all(partial, ('seq', 'grp'), 0, 0, tiled=True)  10.2 us
    ppermute x3, starting transfers between devices, on_device(): lax.ppermute(queries, ('seq', 'grp'), straight(seq, grp, even, odd))  6.9 us
    pallas_call x1, Pallas kernels, on_device(): pl.pallas_call(own_kernel, out_shape=(pltpu.VMEM((KV_HEADS, GROUP, HEAD_D...  1.78 us
    ppermute x1, starting transfers between devices, on_device(): lax.ppermute(queries, ('seq', 'grp'), straight(seq, grp, SHARED, SHARED))  1.58 us
    ppermute x1, waiting for transfers between devices, on_device(): other = lax.ppermute(mine, 'grp', [(j, j ^ 1) for j in range(grp)])  1.18 us
    ppermute x3, waiting for transfers between devices, on_device(): lax.ppermute(queries, ('seq', 'grp'), straight(seq, grp, even, odd))  0.98 us
    pallas_call x1, Pallas kernels, on_device(): pl.pallas_call(functools.partial(partial_kernel, len(every) == 1), out_sh...  0.98 us
    pallas_call x1, Pallas kernels, on_device(): pl.pallas_call(join_kernel, out_shape=jax.ShapeDtypeStruct((1, GROUP * HE...  0.91 us
  transfers between devices with their start and end apart: 5, of which 2 were waited for; matrix products, arithmetic and copies ran while one was open for 0% of the time, Pallas kernels for 7%

profile of v4, /device:TPU:0, one launch (start us, length us, event | category | flops | bytes accessed | tf_op | source)
XLA Modules:
  0.0 25.4 jit_solution(4062181543715605807)
XLA Ops:
  0.0 5.0 %collective-permute-start.1 = (bf16[1,4096]{1,0:T(2,128)(2,1)}, bf16[1,4096]{1,0:T(2,128)(2,1)S(1)}, u32[]{:S(2)}, u32[]{:S(2)}) collective-permute-start(bf16[1,4096]{1,0:T(2,128)(2,1)} %query_ref.1), channel_id=1, source_target_pairs={{0,20},{1,29},{2,22},{3,31},{4,16},{5,25},{6,18},{7,27},{8,28},{9,... | collective-permute-start | bytes 24584 | tf_op jit(solution)/shard_map/ppermute | solution.py:276
  5.0 1.6 %collective-permute-start = (bf16[1,4096]{1,0:T(2,128)(2,1)}, bf16[1,4096]{1,0:T(2,128)(2,1)S(1)}, u32[]{:S(2)}, u32[]{:S(2)}) collective-permute-start(bf16[1,4096]{1,0:T(2,128)(2,1)} %query_ref.1), channel_id=1, source_target_pairs={{0,8},{1,9},{2,10},{3,11},{4,12},{5,13},{6,14},{7,15},{8,0},{9,1},... | collective-permute-start | bytes 24584 | tf_op jit(solution)/shard_map/ppermute | solution.py:278
  6.6 0.5 %collective-permute-start.3 = (bf16[1,4096]{1,0:T(2,128)(2,1)}, bf16[1,4096]{1,0:T(2,128)(2,1)S(1)}, u32[]{:S(2)}, u32[]{:S(2)}) collective-permute-start(bf16[1,4096]{1,0:T(2,128)(2,1)} %query_ref.1), channel_id=1, source_target_pairs={{0,4},{1,25},{2,6},{3,27},{4,0},{5,29},{6,2},{7,31},{8,12},{9,17},... | collective-permute-start | bytes 24584 | tf_op jit(solution)/shard_map/ppermute | solution.py:276
  7.1 1.4 %collective-permute-start.2 = (bf16[1,4096]{1,0:T(2,128)(2,1)}, bf16[1,4096]{1,0:T(2,128)(2,1)S(1)}, u32[]{:S(2)}, u32[]{:S(2)}) collective-permute-start(bf16[1,4096]{1,0:T(2,128)(2,1)} %query_ref.1), channel_id=1, source_target_pairs={{0,12},{1,17},{2,14},{3,19},{4,8},{5,21},{6,10},{7,23},{8,4},{9,25... | collective-permute-start | bytes 24584 | tf_op jit(solution)/shard_map/ppermute | solution.py:276
  9.1 1.8 %shard_map.64 = (f32[4,8,128]{2,1,0:T(8,128)S(1)}, f32[4,8,128]{2,1,0:T(8,128)S(1)}, bf16[32,128]{1,0:T(8,128)(2,1)S(1)}, bf16[1024,512]{1,0:T(8,128)(2,1)S(1)}, bf16[1024,512]{1,0:T(8,128)(2,1)S(1)}) custom-call(s32[1,1]{1,0:T(1,128)} %bitcast.6.lengths_ref, bf16[1,4096]{1,0:T(2,128)(2,1)} %query_ref.1, bf16[256,512]{1,0:T(8,128)(2,1)} %bitcast.9, ...), custom_call_target="tpu_custom_call" | custom-call | tf_op jit(solution)/shard_map/pallas_call | solution.py:247
  10.9 0.0 collective-permute-done.1.refs_0_
  10.9 0.0 collective-permute-done.shared_ref
  10.9 0.0 collective-permute-done.3.refs_2_
  10.9 1.0 %collective-permute-done.2.refs_1_ = bf16[1,4096]{1,0:T(2,128)(2,1)S(1)} collective-permute-done((bf16[1,4096]{1,0:T(2,128)(2,1)}, bf16[1,4096]{1,0:T(2,128)(2,1)S(1)}, u32[]{:S(2)}, u32[]{:S(2)}) %collective-permute-start.2) | collective-permute-done | bytes 8224 | tf_op jit(solution)/shard_map/ppermute | solution.py:276
  12.0 0.1 collective-permute-start.4
  12.0 1.2 %collective-permute-done.4.refs_2_ = bf16[3,32,128]{2,1,0:T(8,128)(2,1)S(1)} collective-permute-done((bf16[3,32,128]{2,1,0:T(8,128)(2,1)S(1)}, bf16[3,32,128]{2,1,0:T(8,128)(2,1)S(1)}, u32[]{:S(2)}, u32[]{:S(2)}) %collective-permute-start.4) | collective-permute-done | bytes 24608 | tf_op jit(solution)/shard_map/ppermute | solution.py:288
  13.2 1.0 %shard_map.66 = f32[320,128]{1,0:T(8,128)S(1)} custom-call(bf16[1024,512]{1,0:T(8,128)(2,1)S(1)} %get-tuple-element.12.key_ref, bf16[1024,512]{1,0:T(8,128)(2,1)S(1)} %get-tuple-element.13.value_ref, f32[4,8,128]{2,1,0:T(8,128)S(1)} %get-tuple-element.14.own_ref, f32[4,8,128]{2,1,0:T(8,128)S(1)} %get-tuple-element.15.own_sums_ref, ...), custom_call_target="tpu_custom_call" | custom-call | tf_op jit(solution)/shard_map/pallas_call | solution.py:299
  14.2 10.2 %all_to_all.5 = f16[32,5,2,128]{3,2,1,0:T(2,128)(2,1)S(1)} all-to-all(f16[32,5,2,128]{3,2,1,0:T(2,128)(2,1)S(1)} %bitcast.7), channel_id=1, replica_groups=mesh['seq'=8,'grp'=4] {'seq','grp'}, dimensions={0} | all-to-all | bytes 163840 | tf_op jit(solution)/shard_map/all_to_all | solution.py:307
  24.5 0.9 %shard_map.67 = bf16[1,1024]{1,0:T(2,128)(2,1)} custom-call(f32[320,128]{1,0:T(8,128)S(1)} %convert.1.parts_ref), custom_call_target="tpu_custom_call" | custom-call | tf_op jit(solution)/shard_map/pallas_call | solution.py:309
  (3 shorter events, 0.1 us)
Async XLA Ops:
  0.0 10.9 %collective-permute-start.1 = (bf16[1,4096]{1,0:T(2,128)(2,1)}, bf16[1,4096]{1,0:T(2,128)(2,1)S(1)}, u32[]{:S(2)}, u32[]{:S(2)}) collective-permute-start(bf16[1,4096]{1,0:T(2,128)(2,1)} %query_ref.1), channel_id=1, source_target_pairs={{0,20},{1,29},{2,22},{3,31},{4,16},{5,25},{6,18},{7,27},{8,28},{9,... | collective-permute-start | bytes 24584 | tf_op jit(solution)/shard_map/ppermute | solution.py:276
  5.0 5.9 %collective-permute-start = (bf16[1,4096]{1,0:T(2,128)(2,1)}, bf16[1,4096]{1,0:T(2,128)(2,1)S(1)}, u32[]{:S(2)}, u32[]{:S(2)}) collective-permute-start(bf16[1,4096]{1,0:T(2,128)(2,1)} %query_ref.1), channel_id=1, source_target_pairs={{0,8},{1,9},{2,10},{3,11},{4,12},{5,13},{6,14},{7,15},{8,0},{9,1},... | collective-permute-start | bytes 24584 | tf_op jit(solution)/shard_map/ppermute | solution.py:278
  6.6 4.4 %collective-permute-start.3 = (bf16[1,4096]{1,0:T(2,128)(2,1)}, bf16[1,4096]{1,0:T(2,128)(2,1)S(1)}, u32[]{:S(2)}, u32[]{:S(2)}) collective-permute-start(bf16[1,4096]{1,0:T(2,128)(2,1)} %query_ref.1), channel_id=1, source_target_pairs={{0,4},{1,25},{2,6},{3,27},{4,0},{5,29},{6,2},{7,31},{8,12},{9,17},... | collective-permute-start | bytes 24584 | tf_op jit(solution)/shard_map/ppermute | solution.py:276
  7.1 4.8 %collective-permute-start.2 = (bf16[1,4096]{1,0:T(2,128)(2,1)}, bf16[1,4096]{1,0:T(2,128)(2,1)S(1)}, u32[]{:S(2)}, u32[]{:S(2)}) collective-permute-start(bf16[1,4096]{1,0:T(2,128)(2,1)} %query_ref.1), channel_id=1, source_target_pairs={{0,12},{1,17},{2,14},{3,19},{4,8},{5,21},{6,10},{7,23},{8,4},{9,25... | collective-permute-start | bytes 24584 | tf_op jit(solution)/shard_map/ppermute | solution.py:276
  12.0 1.3 %collective-permute-start.4 = (bf16[3,32,128]{2,1,0:T(8,128)(2,1)S(1)}, bf16[3,32,128]{2,1,0:T(8,128)(2,1)S(1)}, u32[]{:S(2)}, u32[]{:S(2)}) collective-permute-start(bf16[3,32,128]{2,1,0:T(8,128)(2,1)S(1)} %get-tuple-element.18.refs_1_), channel_id=1, source_target_pairs={{0,1},{1,0},{2,3},{3,2},{4,5},{5,4},{6,7},{7,6},{8,9},{9,8},{10,11... | collective-permute-start | bytes 73736 | tf_op jit(solution)/shard_map/ppermute | solution.py:288

commit v5 on v4

--- a/solution.py
+++ b/solution.py
@@ -19,17 +19,24 @@
 ROWS = GROUP + 2
 SHARED = 2
 DIRECT = ((5, 7), (3, 4), (1, 6))
+ORDER = (1, 0, 3, 2)
 COARSE = 8.0
 SCALE = 1.0 / math.sqrt(HEAD_DIM)
 LOWEST = -1e30
+LIMIT = pltpu.CompilerParams(vmem_limit_bytes=24 << 20)
 SMALLEST = 2.0**-120
 
 VMEM = pl.BlockSpec(memory_space=pltpu.VMEM)
+HBM = pl.BlockSpec(memory_space=pltpu.HBM)
 ANY = pl.BlockSpec(memory_space=pl.ANY)
 
 
 def in_vmem(x):
     return pltpu.with_memory_space_constraint(x, pltpu.VMEM)
+
+
+def in_hbm(x):
+    return pltpu.with_memory_space_constraint(x, pltpu.HBM)
 
 
 def head_rows(query_ref):
@@ -42,12 +49,14 @@
     out_ref[...] = jnp.broadcast_to(head_rows(query_ref)[None], out_ref.shape)
 
 
-def collect_kernel(own_ref, shared_ref, *refs):
-    *direct_refs, near_ref, mine_ref = refs
-    near_ref[0] = own_ref[...]
-    near_ref[1] = head_rows(shared_ref)
-    for i, ref in enumerate(direct_refs):
-        mine_ref[i] = head_rows(ref)
+def collect_kernel(own_ref, *refs):
+    *in_refs, near_ref, mine_ref = refs
+    near_ref[0] = own_ref[0]
+    for i, ref in zip(ORDER, in_refs):
+        if i == len(DIRECT):
+            near_ref[1] = head_rows(ref)
+        else:
+            mine_ref[i] = head_rows(ref)
 
 
 def dot_rows(a, b):
@@ -68,36 +77,50 @@
     return out
 
 
-def own_kernel(
-    lengths_ref, query_ref, own_key_ref, own_value_ref, key_ref, value_ref,
-    own_ref, sums_ref, rows_ref, key_out, value_out,
-    length, query_buf, own_key, own_value, sems,
+def load_kernel(
+    query_ref, lengths_ref, own_key_ref, own_value_ref, key_ref, value_ref,
+    rows_ref, length_ref, own_key_out, own_value_out, key_out, value_out,
+    query, length, key, sems,
 ):
     moves = (
-        (query_ref, query_buf),
-        (own_key_ref, own_key),
+        (query_ref, query),
+        (key_ref, key),
         (lengths_ref, length),
-        (own_value_ref, own_value),
+        (own_key_ref, own_key_out),
+        (own_value_ref, own_value_out),
         (value_ref, value_out),
-        (key_ref, key_out),
     )
     moves = [pltpu.make_async_copy(a, b, sems.at[i]) for i, (a, b) in enumerate(moves)]
     for move in moves:
         move.start()
-    span = own_key.shape[0]
+    moves[0].wait()
+    rows_ref[0] = head_rows(query)
+    moves[1].wait()
+    key_out[...] = key[...].T
+    moves[2].wait()
+    length_ref[...] = jnp.broadcast_to(length[...], length_ref.shape)
+    for move in moves[3:]:
+        move.wait()
+
+
+def own_kernel(
+    length_ref, query_ref, own_key_ref, own_value_ref, value_ref, own_ref, sums_ref
+):
+    span = own_key_ref.shape[0]
     position = lax.broadcasted_iota(jnp.int32, (2 * GROUP, span), 1) + lax.axis_index("grp") * span
-    moves[0].wait()
-    rows_ref[...] = head_rows(query_buf)
-    query = rows_ref[...].astype(jnp.float32)
-    moves[1].wait()
+    live = position < length_ref[:1, :1]
+    query = query_ref[0].astype(jnp.float32)
     scores = []
     for i in range(PAIRS):
         top = 2 * i * GROUP
         both = side_by_side(query[top : top + GROUP], query[top + GROUP : top + 2 * GROUP])
-        scores.append(dot_rows(both, own_key[:, i * PAIR_DIM : (i + 1) * PAIR_DIM]))
-    moves[2].wait()
-    live = position < length[...]
-    moves[3].wait()
+        scores.append(dot_rows(both, own_key_ref[:, i * PAIR_DIM : (i + 1) * PAIR_DIM]))
+    largest = jnp.max(jnp.abs(value_ref[...]), axis=0, keepdims=True)
+    largest = jnp.maximum(largest, jnp.max(jnp.abs(own_value_ref[...]), axis=0, keepdims=True))
+    largest = jnp.max(largest.astype(jnp.float32), axis=1, keepdims=True)
+    power = jnp.ceil(jnp.log2(jnp.maximum(largest, SMALLEST)))
+    power -= 15 - (value_ref.shape[0] + span - 1).bit_length()
+    shrink = jnp.exp2(-power)
     peaks, totals = [], []
     for i in range(PAIRS):
         masked = jnp.where(live, scores[i], LOWEST)
@@ -106,27 +129,17 @@
         total = jnp.sum(expo, axis=1, keepdims=True)
         output = jnp.dot(
             expo.astype(jnp.bfloat16),
-            own_value[:, i * PAIR_DIM : (i + 1) * PAIR_DIM],
+            own_value_ref[:, i * PAIR_DIM : (i + 1) * PAIR_DIM],
             preferred_element_type=jnp.float32,
         )
-        own_ref[2 * i] = output[:GROUP, :HEAD_DIM]
-        own_ref[2 * i + 1] = output[GROUP:, HEAD_DIM:]
+        own_ref[2 * i] = output[:GROUP, :HEAD_DIM] * shrink
+        own_ref[2 * i + 1] = output[GROUP:, HEAD_DIM:] * shrink
         peaks += [peak[:GROUP], peak[GROUP:]]
         totals += [total[:GROUP], total[GROUP:]]
-    largest = jnp.max(jnp.abs(own_value[...]), axis=0, keepdims=True)
-    moves[4].wait()
-    largest = jnp.maximum(largest, jnp.max(jnp.abs(value_out[...]), axis=0, keepdims=True))
-    largest = jnp.max(largest.astype(jnp.float32), axis=1, keepdims=True)
-    power = jnp.ceil(jnp.log2(jnp.maximum(largest, SMALLEST)))
-    power -= 15 - (key_ref.shape[0] + span - 1).bit_length()
-    shrink = jnp.exp2(-power)
-    for j in range(KV_HEADS):
-        own_ref[j] *= shrink
     sums_ref[0] = in_lanes(peaks, GROUP)
     sums_ref[1] = in_lanes(totals, GROUP)
     sums_ref[2] = jnp.broadcast_to(power * (math.log(2.0) / SCALE), (GROUP, HEAD_DIM))
     sums_ref[3] = jnp.broadcast_to(shrink, (GROUP, HEAD_DIM))
-    moves[5].wait()
 
 
 def partial_kernel(
@@ -169,9 +182,10 @@
             for j in range(KV_HEADS)
         ]
         scores = [
-            dot_rows(
+            jnp.dot(
                 side_by_side(heads[2 * i], heads[2 * i + 1]),
-                key_ref[:, i * PAIR_DIM : (i + 1) * PAIR_DIM],
+                key_ref[i * PAIR_DIM : (i + 1) * PAIR_DIM],
+                preferred_element_type=jnp.float32,
             )
             for i in range(PAIRS)
         ]
@@ -244,31 +258,32 @@
 def on_device(seq, grp, queries, prompt_keys, prompt_values, suffix_keys, suffix_values, lengths):
     span = suffix_keys.shape[1]
     width = KV_HEADS * HEAD_DIM
-    own, own_sums, rows, keys, values = pl.pallas_call(
-        own_kernel,
+    rows, length, own_keys, own_values, keys, values = pl.pallas_call(
+        load_kernel,
+        compiler_params=LIMIT,
         out_shape=(
-            pltpu.VMEM((KV_HEADS, GROUP, HEAD_DIM), jnp.float32),
-            pltpu.VMEM((4, GROUP, HEAD_DIM), jnp.float32),
-            pltpu.VMEM((Q_HEADS, HEAD_DIM), queries.dtype),
-            pltpu.VMEM(prompt_keys.shape, prompt_keys.dtype),
+            pltpu.VMEM((1, Q_HEADS, HEAD_DIM), queries.dtype),
+            pltpu.VMEM((GROUP, HEAD_DIM), jnp.int32),
+            pltpu.VMEM((span, width), suffix_keys.dtype),
+            pltpu.VMEM((span, width), suffix_values.dtype),
+            pltpu.VMEM(prompt_keys.shape[::-1], prompt_keys.dtype),
             pltpu.VMEM(prompt_values.shape, prompt_values.dtype),
         ),
-        in_specs=[ANY] * 6,
-        out_specs=(VMEM,) * 5,
+        in_specs=[HBM, ANY] + [HBM] * 4,
+        out_specs=(VMEM,) * 6,
         scratch_shapes=[
+            pltpu.VMEM(queries.shape, queries.dtype),
             pltpu.VMEM((1, 1), jnp.int32),
-            pltpu.VMEM(queries.shape, queries.dtype),
-            pltpu.VMEM((span, width), suffix_keys.dtype),
-            pltpu.VMEM((span, width), suffix_values.dtype),
+            pltpu.VMEM(prompt_keys.shape, prompt_keys.dtype),
             pltpu.SemaphoreType.DMA((6,)),
         ],
     )(
+        in_hbm(queries),
         lengths.reshape(1, 1),
-        queries,
-        suffix_keys.reshape(span, width),
-        suffix_values.reshape(span, width),
-        prompt_keys,
-        prompt_values,
+        in_hbm(suffix_keys.reshape(span, width)),
+        in_hbm(suffix_values.reshape(span, width)),
+        in_hbm(prompt_keys),
+        in_hbm(prompt_values),
     )
     scratch = [pltpu.VMEM((2 * BLOCK_ROWS, HEAD_DIM), jnp.float32)]
     if seq == BLOCK and grp % 2 == 0:
@@ -278,26 +293,39 @@
         shared = lax.ppermute(queries, ("seq", "grp"), straight(seq, grp, SHARED, SHARED))
         near, mine = pl.pallas_call(
             collect_kernel,
+            compiler_params=LIMIT,
             out_shape=(
                 pltpu.VMEM((2, Q_HEADS, HEAD_DIM), queries.dtype),
                 pltpu.VMEM((len(DIRECT), Q_HEADS, HEAD_DIM), queries.dtype),
             ),
             in_specs=[VMEM] * (2 + len(DIRECT)),
             out_specs=(VMEM, VMEM),
-        )(in_vmem(rows), in_vmem(shared), *map(in_vmem, direct))
+        )(in_vmem(rows), *[in_vmem([*direct, shared][i]) for i in ORDER])
         other = lax.ppermute(mine, "grp", [(j, j ^ 1) for j in range(grp)])
-        every = [near, mine, other]
+        own_rows, every = near, [near, mine, other]
         scratch.append(pltpu.VMEM((seq, Q_HEADS, HEAD_DIM), queries.dtype))
     else:
         copies = pl.pallas_call(
             spread_kernel,
+            compiler_params=LIMIT,
             out_shape=pltpu.VMEM((seq, Q_HEADS, HEAD_DIM), queries.dtype),
             in_specs=[VMEM],
             out_specs=VMEM,
         )(queries)
-        every = [lax.all_to_all(copies, "seq", 0, 0, tiled=True)]
+        own_rows, every = rows, [lax.all_to_all(copies, "seq", 0, 0, tiled=True)]
+    own, own_sums = pl.pallas_call(
+        own_kernel,
+        compiler_params=LIMIT,
+        out_shape=(
+            pltpu.VMEM((KV_HEADS, GROUP, HEAD_DIM), jnp.float32),
+            pltpu.VMEM((4, GROUP, HEAD_DIM), jnp.float32),
+        ),
+        in_specs=[VMEM] * 5,
+        out_specs=(VMEM, VMEM),
+    )(*map(in_vmem, (length, own_rows, own_keys, own_values, values)))
     partial = pl.pallas_call(
         functools.partial(partial_kernel, len(every) == 1),
+        compiler_params=LIMIT,
         out_shape=pltpu.VMEM((seq * grp * ROWS, HEAD_DIM), jnp.float32),
         in_specs=[VMEM] * (4 + len(every)),
         out_specs=VMEM,
@@ -308,6 +336,7 @@
     parts = parts.astype(jnp.float32).reshape(seq * grp * ROWS, HEAD_DIM)
     return pl.pallas_call(
         join_kernel,
+        compiler_params=LIMIT,
         out_shape=jax.ShapeDtypeStruct((1, GROUP * HEAD_DIM), queries.dtype),
         in_specs=[VMEM],
         out_specs=VMEM,

time: 25.7 us -> 24.6 us (0.957)
  blocking collectives: 10.2 us -> 9.3 us
  waiting for transfers between devices: 2.17 us -> 1.78 us
  Pallas kernels: 3.71 us -> 3.99 us
    ppermute x3, starting transfers between devices: 6.9 us -> 8.03 us  [on_device(): lax.ppermute(queries, ('seq', 'grp'), straight(seq, grp, even, odd))]
    ppermute x1, starting transfers between devices: 1.58 us -> 0.45 us  [on_device(): lax.ppermute(queries, ('seq', 'grp'), straight(seq, grp, SHARED, SHARED))]
    ppermute x1, waiting for transfers between devices: 0.01 us -> 1.04 us  [on_device(): lax.ppermute(queries, ('seq', 'grp'), straight(seq, grp, SHARED, SHARED))]
    ppermute x3, waiting for transfers between devices: 0.98 us -> 0.01 us  [on_device(): lax.ppermute(queries, ('seq', 'grp'), straight(seq, grp, even, odd))]
    all_to_all x1, blocking collectives: 10.2 us -> 9.3 us  [on_device(): parts = lax.all_to_all(partial, ('seq', 'grp'), 0, 0, tiled=True)]
    ppermute x1, waiting for transfers between devices: 1.18 us -> 0.73 us  [on_device(): other = lax.ppermute(mine, 'grp', [(j, j ^ 1) for j in range(grp)])]
    pallas_call x4 -> x5, Pallas kernels: 3.71 us -> 3.99 us  [the longest x1 1.77 us: on_device(): pl.pallas_call(load_kernel, compiler_params=LIMIT, out_shape=(pltpu.VMEM(...]
  transfers between devices with their start and end apart: 5 -> 5, of which waited for: 2 -> 2; matrix products, arithmetic and copies ran while one was open for 0% -> 0% of each run, Pallas kernels for 7% -> 9%
where the time goes in v5:
time: 24.6 us; the launch traced here: 24.4 us
  blocking collectives  9.3 us (38%)
  starting transfers between devices  8.55 us (35%)
  Pallas kernels  3.99 us (16%)
  waiting for transfers between devices  1.78 us (7%)
  between operations  0.72 us (3%)
    all_to_all x1, blocking collectives, on_device(): parts = lax.all_to_all(partial, ('seq', 'grp'), 0, 0, tiled=True)  9.3 us
    ppermute x3, starting transfers between devices, on_device(): lax.ppermute(queries, ('seq', 'grp'), straight(seq, grp, even, odd))  8.03 us
    pallas_call x1, Pallas kernels, on_device(): pl.pallas_call(load_kernel, compiler_params=LIMIT, out_shape=(pltpu.VMEM(...  1.77 us
    ppermute x1, waiting for transfers between devices, on_device(): lax.ppermute(queries, ('seq', 'grp'), straight(seq, grp, SHARED, SHARED))  1.04 us
    pallas_call x1, Pallas kernels, on_device(): pl.pallas_call(join_kernel, compiler_params=LIMIT, out_shape=jax.ShapeDty...  0.91 us
    pallas_call x1, Pallas kernels, on_device(): pl.pallas_call(functools.partial(partial_kernel, len(every) == 1), compil...  0.82 us
    ppermute x1, waiting for transfers between devices, on_device(): other = lax.ppermute(mine, 'grp', [(j, j ^ 1) for j in range(grp)])  0.73 us
  transfers between devices with their start and end apart: 5, of which 2 were waited for; matrix products, arithmetic and copies ran while one was open for 0% of the time, Pallas kernels for 9%

profile of v5, /device:TPU:0, one launch (start us, length us, event | category | flops | bytes accessed | tf_op | source)
XLA Modules:
  0.0 24.4 jit_solution(8736967601069131756)
XLA Ops:
  0.0 5.0 %collective-permute-start.1 = (bf16[1,4096]{1,0:T(2,128)(2,1)}, bf16[1,4096]{1,0:T(2,128)(2,1)S(1)}, u32[]{:S(2)}, u32[]{:S(2)}) collective-permute-start(bf16[1,4096]{1,0:T(2,128)(2,1)} %query_ref.1), channel_id=1, source_target_pairs={{0,20},{1,29},{2,22},{3,31},{4,16},{5,25},{6,18},{7,27},{8,28},{9,... | collective-permute-start | bytes 24584 | tf_op jit(solution)/shard_map/ppermute | solution.py:291
  5.0 1.5 %collective-permute-start = (bf16[1,4096]{1,0:T(2,128)(2,1)}, bf16[1,4096]{1,0:T(2,128)(2,1)S(1)}, u32[]{:S(2)}, u32[]{:S(2)}) collective-permute-start(bf16[1,4096]{1,0:T(2,128)(2,1)} %query_ref.1), channel_id=1, source_target_pairs={{0,12},{1,17},{2,14},{3,19},{4,8},{5,21},{6,10},{7,23},{8,4},{9,25... | collective-permute-start | bytes 24584 | tf_op jit(solution)/shard_map/ppermute | solution.py:291
  6.5 1.5 %collective-permute-start.3 = (bf16[1,4096]{1,0:T(2,128)(2,1)}, bf16[1,4096]{1,0:T(2,128)(2,1)S(1)}, u32[]{:S(2)}, u32[]{:S(2)}) collective-permute-start(bf16[1,4096]{1,0:T(2,128)(2,1)} %query_ref.1), channel_id=1, source_target_pairs={{0,4},{1,25},{2,6},{3,27},{4,0},{5,29},{6,2},{7,31},{8,12},{9,17},... | collective-permute-start | bytes 24584 | tf_op jit(solution)/shard_map/ppermute | solution.py:291
  8.0 0.4 %collective-permute-start.2 = (bf16[1,4096]{1,0:T(2,128)(2,1)}, bf16[1,4096]{1,0:T(2,128)(2,1)S(1)}, u32[]{:S(2)}, u32[]{:S(2)}) collective-permute-start(bf16[1,4096]{1,0:T(2,128)(2,1)} %query_ref.1), channel_id=1, source_target_pairs={{0,8},{1,9},{2,10},{3,11},{4,12},{5,13},{6,14},{7,15},{8,0},{9,1},... | collective-permute-start | bytes 24584 | tf_op jit(solution)/shard_map/ppermute | solution.py:293
  9.1 1.8 %shard_map.64 = (bf16[1,32,128]{2,1,0:T(8,128)(2,1)S(1)}, s32[8,128]{1,0:T(8,128)S(1)}, bf16[256,512]{1,0:T(8,128)(2,1)S(1)}, bf16[256,512]{1,0:T(8,128)(2,1)S(1...) custom-call(bf16[1,4096]{1,0:T(2,128)(2,1)} %query_ref.1, s32[1,1]{1,0:T(1,128)} %bitcast.6.lengths_ref, ...), custom_call_target="tpu_custom_call" | custom-call | tf_op jit(solution)/shard_map/pallas_call | solution.py:261
  10.9 0.0 collective-permute-done.1.refs_1_
  10.9 0.0 collective-permute-done.refs_0_
  10.9 0.0 collective-permute-done.3.refs_3_
  10.9 1.0 %collective-permute-done.2.refs_2_ = bf16[1,4096]{1,0:T(2,128)(2,1)S(1)} collective-permute-done((bf16[1,4096]{1,0:T(2,128)(2,1)}, bf16[1,4096]{1,0:T(2,128)(2,1)S(1)}, u32[]{:S(2)}, u32[]{:S(2)}) %collective-permute-start.2) | collective-permute-done | bytes 8224 | tf_op jit(solution)/shard_map/ppermute | solution.py:293
  12.0 0.1 collective-permute-start.4
  12.1 0.4 %shard_map.66 = (f32[4,8,128]{2,1,0:T(8,128)S(1)}, f32[4,8,128]{2,1,0:T(8,128)S(1)}) custom-call(s32[8,128]{1,0:T(8,128)S(1)} %get-tuple-element.17.length_ref, bf16[2,32,128]{2,1,0:T(8,128)(2,1)S(1)} %get-tuple-element.19.query_ref.refs_0_, bf16[256,512]{1,0:T(8,128)(2,1)S(1)} %get-tuple-element.20.own_key_ref, ...), custom_call_target="tpu_custom_call" | custom-call | tf_op jit(solution)/shard_map/pallas_call | solution.py:316
  12.6 0.7 %collective-permute-done.4.refs_2_ = bf16[3,32,128]{2,1,0:T(8,128)(2,1)S(1)} collective-permute-done((bf16[3,32,128]{2,1,0:T(8,128)(2,1)S(1)}, bf16[3,32,128]{2,1,0:T(8,128)(2,1)S(1)}, u32[]{:S(2)}, u32[]{:S(2)}) %collective-permute-start.4) | collective-permute-done | bytes 24608 | tf_op jit(solution)/shard_map/ppermute | solution.py:304
  13.3 0.8 %shard_map.67 = f32[320,128]{1,0:T(8,128)S(1)} custom-call(bf16[512,1024]{1,0:T(8,128)(2,1)S(1)} %get-tuple-element.15.key_ref, bf16[1024,512]{1,0:T(8,128)(2,1)S(1)} %get-tuple-element.16.value_ref, f32[4,8,128]{2,1,0:T(8,128)S(1)} %get-tuple-element.22.own_ref, f32[4,8,128]{2,1,0:T(8,128)S(1)} %get-tuple-element.23.own_sums_ref, ...), custom_call_target="tpu_custom_call" | custom-call | tf_op jit(solution)/shard_map/pallas_call | solution.py:326
  14.1 9.3 %all_to_all.5 = f16[32,5,2,128]{3,2,1,0:T(2,128)(2,1)S(1)} all-to-all(f16[32,5,2,128]{3,2,1,0:T(2,128)(2,1)S(1)} %bitcast.7), channel_id=1, replica_groups=mesh['seq'=8,'grp'=4] {'seq','grp'}, dimensions={0} | all-to-all | bytes 163840 | tf_op jit(solution)/shard_map/all_to_all | solution.py:335
  23.5 0.9 %shard_map.68 = bf16[1,1024]{1,0:T(2,128)(2,1)} custom-call(f32[320,128]{1,0:T(8,128)S(1)} %convert.1.parts_ref), custom_call_target="tpu_custom_call" | custom-call | tf_op jit(solution)/shard_map/pallas_call | solution.py:337
  (3 shorter events, 0.1 us)
Async XLA Ops:
  0.0 10.9 %collective-permute-start.1 = (bf16[1,4096]{1,0:T(2,128)(2,1)}, bf16[1,4096]{1,0:T(2,128)(2,1)S(1)}, u32[]{:S(2)}, u32[]{:S(2)}) collective-permute-start(bf16[1,4096]{1,0:T(2,128)(2,1)} %query_ref.1), channel_id=1, source_target_pairs={{0,20},{1,29},{2,22},{3,31},{4,16},{5,25},{6,18},{7,27},{8,28},{9,... | collective-permute-start | bytes 24584 | tf_op jit(solution)/shard_map/ppermute | solution.py:291
  5.0 5.9 %collective-permute-start = (bf16[1,4096]{1,0:T(2,128)(2,1)}, bf16[1,4096]{1,0:T(2,128)(2,1)S(1)}, u32[]{:S(2)}, u32[]{:S(2)}) collective-permute-start(bf16[1,4096]{1,0:T(2,128)(2,1)} %query_ref.1), channel_id=1, source_target_pairs={{0,12},{1,17},{2,14},{3,19},{4,8},{5,21},{6,10},{7,23},{8,4},{9,25... | collective-permute-start | bytes 24584 | tf_op jit(solution)/shard_map/ppermute | solution.py:291
  6.5 4.4 %collective-permute-start.3 = (bf16[1,4096]{1,0:T(2,128)(2,1)}, bf16[1,4096]{1,0:T(2,128)(2,1)S(1)}, u32[]{:S(2)}, u32[]{:S(2)}) collective-permute-start(bf16[1,4096]{1,0:T(2,128)(2,1)} %query_ref.1), channel_id=1, source_target_pairs={{0,4},{1,25},{2,6},{3,27},{4,0},{5,29},{6,2},{7,31},{8,12},{9,17},... | collective-permute-start | bytes 24584 | tf_op jit(solution)/shard_map/ppermute | solution.py:291
  8.0 3.9 %collective-permute-start.2 = (bf16[1,4096]{1,0:T(2,128)(2,1)}, bf16[1,4096]{1,0:T(2,128)(2,1)S(1)}, u32[]{:S(2)}, u32[]{:S(2)}) collective-permute-start(bf16[1,4096]{1,0:T(2,128)(2,1)} %query_ref.1), channel_id=1, source_target_pairs={{0,8},{1,9},{2,10},{3,11},{4,12},{5,13},{6,14},{7,15},{8,0},{9,1},... | collective-permute-start | bytes 24584 | tf_op jit(solution)/shard_map/ppermute | solution.py:293
  12.0 1.3 %collective-permute-start.4 = (bf16[3,32,128]{2,1,0:T(8,128)(2,1)S(1)}, bf16[3,32,128]{2,1,0:T(8,128)(2,1)S(1)}, u32[]{:S(2)}, u32[]{:S(2)}) collective-permute-start(bf16[3,32,128]{2,1,0:T(8,128)(2,1)S(1)} %get-tuple-element.24.refs_1_), channel_id=1, source_target_pairs={{0,1},{1,0},{2,3},{3,2},{4,5},{5,4},{6,7},{7,6},{8,9},{9,8},{10,11... | collective-permute-start | bytes 73736 | tf_op jit(solution)/shard_map/ppermute | solution.py:304

commit v6 on v5

--- a/solution.py
+++ b/solution.py
@@ -75,6 +75,11 @@
     for j, column in enumerate(columns):
         out = jnp.where(lane == j, column, out)
     return out
+
+
+def both_halves(sums):
+    lane = lax.broadcasted_iota(jnp.int32, sums.shape, 1)
+    return jnp.where(lane < BLOCK_ROWS, sums, pltpu.roll(sums, BLOCK_ROWS, 1))
 
 
 def load_kernel(
@@ -104,7 +109,7 @@
 
 
 def own_kernel(
-    length_ref, query_ref, own_key_ref, own_value_ref, value_ref, own_ref, sums_ref
+    length_ref, query_ref, own_key_ref, own_value_ref, value_ref, own_ref, sums_ref, flat_ref, wide_ref
 ):
     span = own_key_ref.shape[0]
     position = lax.broadcasted_iota(jnp.int32, (2 * GROUP, span), 1) + lax.axis_index("grp") * span
@@ -140,10 +145,17 @@
     sums_ref[1] = in_lanes(totals, GROUP)
     sums_ref[2] = jnp.broadcast_to(power * (math.log(2.0) / SCALE), (GROUP, HEAD_DIM))
     sums_ref[3] = jnp.broadcast_to(shrink, (GROUP, HEAD_DIM))
+    row = (lax.axis_index("seq") % BLOCK) * GROUP
+    wide_ref[:BLOCK_ROWS] = jnp.full((BLOCK_ROWS, HEAD_DIM), LOWEST, jnp.float32)
+    wide_ref[BLOCK_ROWS:] = jnp.zeros((BLOCK_ROWS, HEAD_DIM), jnp.float32)
+    wide_ref[pl.ds(row, GROUP)] = sums_ref[0]
+    wide_ref[pl.ds(BLOCK_ROWS + row, GROUP)] = sums_ref[1]
+    flat_ref[0] = wide_ref[...].T[:GROUP]
+    flat_ref[1] = both_halves(flat_ref[0])
 
 
 def partial_kernel(
-    gathered, key_ref, value_ref, own_ref, own_sums_ref, *refs
+    gathered, key_ref, value_ref, own_ref, own_sums_ref, own_flat_ref, *refs
 ):
     me = lax.axis_index("seq")
     if gathered:
@@ -164,13 +176,10 @@
 
     def join_own():
         row = (me % BLOCK) * GROUP
-        peak, total = sums_ref[pl.ds(row, GROUP)], sums_ref[pl.ds(BLOCK_ROWS + row, GROUP)]
-        own_peak, own_total = own_sums_ref[0], own_sums_ref[1]
+        peak, own_peak = sums_ref[pl.ds(row, GROUP)], own_sums_ref[0]
         joined = jnp.maximum(peak, own_peak)
         factor = jnp.exp((peak - joined) * SCALE)
         own_factor = jnp.exp((own_peak - joined) * SCALE)
-        sums_ref[pl.ds(row, GROUP)] = joined
-        sums_ref[pl.ds(BLOCK_ROWS + row, GROUP)] = total * factor + own_total * own_factor
         for j in range(KV_HEADS):
             rows = pl.ds((me * KV_HEADS + j) * ROWS, GROUP)
             out_ref[rows] = out_ref[rows] * factor[:, j : j + 1] + own_ref[j] * own_factor[:, j : j + 1]
@@ -208,15 +217,21 @@
             totals += [total[:BLOCK_ROWS], total[BLOCK_ROWS:]]
         sums_ref[:BLOCK_ROWS] = in_lanes(peaks, BLOCK_ROWS)
         sums_ref[BLOCK_ROWS:] = in_lanes(totals, BLOCK_ROWS)
+        sums = sums_ref[...].T[:GROUP]
         if count == BLOCK:
             join_own()
         else:
             pl.when(me // BLOCK == block)(join_own)
-        sums = sums_ref[...].T[:GROUP]
+        here = me // BLOCK == block
+        own_peaks = jnp.where(here, own_flat_ref[1], LOWEST)
+        own_totals = jnp.where(here, own_flat_ref[0], 0.0)
+        peaks = both_halves(sums)
+        joined = jnp.maximum(peaks, own_peaks)
+        totals = sums * jnp.exp((peaks - joined) * SCALE)
+        totals += own_totals * jnp.exp((own_peaks - joined) * SCALE)
         lane = lax.broadcasted_iota(jnp.int32, (GROUP, HEAD_DIM), 1)
-        peaks = jnp.where(lane < BLOCK_ROWS, sums, pltpu.roll(sums, BLOCK_ROWS, 1))
-        weights = peaks + jnp.where(
-            lane < BLOCK_ROWS, own_sums_ref[2], jnp.log(sums) * (1.0 / SCALE)
+        weights = joined + jnp.where(
+            lane < BLOCK_ROWS, own_sums_ref[2], jnp.log(totals) * (1.0 / SCALE)
         )
         coarse = jnp.round(weights * (1.0 / COARSE)) * COARSE
         fine = weights - coarse
@@ -238,14 +253,16 @@
     def every(row):
         return parts_ref[pl.ds(row, parts, stride=ROWS)]
 
-    offset = (lax.axis_index("seq") % BLOCK) * GROUP
-    weights = pltpu.roll(every(GROUP) + every(GROUP + 1), (HEAD_DIM - offset) % HEAD_DIM, 1)
+    weights = every(GROUP) + every(GROUP + 1)
     totals = pltpu.roll(weights, HEAD_DIM - BLOCK_ROWS, 1)
     top = jnp.max(totals, axis=0, keepdims=True)
     total = jnp.sum(jnp.exp((totals - top) * SCALE), axis=0, keepdims=True)
     factor = jnp.exp((weights - top) * SCALE) / total
+    first = (lax.axis_index("seq") % BLOCK) * GROUP
     for h in range(GROUP):
-        output = jnp.sum(every(h) * factor[:, h : h + 1], axis=0, keepdims=True)
+        lane = jnp.full(factor.shape, first + h, jnp.int32)
+        output = every(h) * jnp.take_along_axis(factor, lane, axis=1)
+        output = jnp.sum(output, axis=0, keepdims=True)
         out_ref[:, h * HEAD_DIM : (h + 1) * HEAD_DIM] = output.astype(out_ref.dtype)
 
 
@@ -313,24 +330,26 @@
             out_specs=VMEM,
         )(queries)
         own_rows, every = rows, [lax.all_to_all(copies, "seq", 0, 0, tiled=True)]
-    own, own_sums = pl.pallas_call(
+    own, own_sums, own_flat = pl.pallas_call(
         own_kernel,
         compiler_params=LIMIT,
         out_shape=(
             pltpu.VMEM((KV_HEADS, GROUP, HEAD_DIM), jnp.float32),
             pltpu.VMEM((4, GROUP, HEAD_DIM), jnp.float32),
+            pltpu.VMEM((2, GROUP, HEAD_DIM), jnp.float32),
         ),
         in_specs=[VMEM] * 5,
-        out_specs=(VMEM, VMEM),
+        out_specs=(VMEM,) * 3,
+        scratch_shapes=[pltpu.VMEM((2 * BLOCK_ROWS, HEAD_DIM), jnp.float32)],
     )(*map(in_vmem, (length, own_rows, own_keys, own_values, values)))
     partial = pl.pallas_call(
         functools.partial(partial_kernel, len(every) == 1),
         compiler_params=LIMIT,
         out_shape=pltpu.VMEM((seq * grp * ROWS, HEAD_DIM), jnp.float32),
-        in_specs=[VMEM] * (4 + len(every)),
+        in_specs=[VMEM] * (5 + len(every)),
         out_specs=VMEM,
         scratch_shapes=scratch,
-    )(in_vmem(keys), in_vmem(values), in_vmem(own), in_vmem(own_sums), *map(in_vmem, every))
+    )(in_vmem(keys), in_vmem(values), *map(in_vmem, (own, own_sums, own_flat, *every)))
     partial = partial.reshape(seq * grp, ROWS // 2, 2, HEAD_DIM).astype(jnp.float16)
     parts = lax.all_to_all(partial, ("seq", "grp"), 0, 0, tiled=True)
     parts = parts.astype(jnp.float32).reshape(seq * grp * ROWS, HEAD_DIM)

time: 24.6 us -> 24.5 us (level)
  no operation moved by 1% of the time
where the time goes in v6:
time: 24.5 us; the launch traced here: 24.3 us
  blocking collectives  9.3 us (38%)
  starting transfers between devices  8.55 us (35%)
  Pallas kernels  3.94 us (16%)
  waiting for transfers between devices  1.73 us (7%)
  between operations  0.72 us (3%)
    all_to_all x1, blocking collectives, on_device(): parts = lax.all_to_all(partial, ('seq', 'grp'), 0, 0, tiled=True)  9.3 us
    ppermute x3, starting transfers between devices, on_device(): lax.ppermute(queries, ('seq', 'grp'), straight(seq, grp, even, odd))  8.03 us
    pallas_call x1, Pallas kernels, on_device(): pl.pallas_call(load_kernel, compiler_params=LIMIT, out_shape=(pltpu.VMEM(...  1.77 us
    ppermute x1, waiting for transfers between devices, on_device(): lax.ppermute(queries, ('seq', 'grp'), straight(seq, grp, SHARED, SHARED))  1.04 us
    pallas_call x1, Pallas kernels, on_device(): pl.pallas_call(join_kernel, compiler_params=LIMIT, out_shape=jax.ShapeDty...  0.85 us
    pallas_call x1, Pallas kernels, on_device(): pl.pallas_call(functools.partial(partial_kernel, len(every) == 1), compil...  0.78 us
    ppermute x1, waiting for transfers between devices, on_device(): other = lax.ppermute(mine, 'grp', [(j, j ^ 1) for j in range(grp)])  0.68 us
    pallas_call x1, Pallas kernels, on_device(): pl.pallas_call(own_kernel, compiler_params=LIMIT, out_shape=(pltpu.VMEM((...  0.5 us
  transfers between devices with their start and end apart: 5, of which 2 were waited for; matrix products, arithmetic and copies ran while one was open for 0% of the time, Pallas kernels for 9%

profile of v6, /device:TPU:0, one launch (start us, length us, event | category | flops | bytes accessed | tf_op | source)
XLA Modules:
  0.0 24.3 jit_solution(6799125456385947326)
XLA Ops:
  0.0 5.0 %collective-permute-start.1 = (bf16[1,4096]{1,0:T(2,128)(2,1)}, bf16[1,4096]{1,0:T(2,128)(2,1)S(1)}, u32[]{:S(2)}, u32[]{:S(2)}) collective-permute-start(bf16[1,4096]{1,0:T(2,128)(2,1)} %query_ref.1), channel_id=1, source_target_pairs={{0,20},{1,29},{2,22},{3,31},{4,16},{5,25},{6,18},{7,27},{8,28},{9,... | collective-permute-start | bytes 24584 | tf_op jit(solution)/shard_map/ppermute | solution.py:308
  5.0 1.5 %collective-permute-start = (bf16[1,4096]{1,0:T(2,128)(2,1)}, bf16[1,4096]{1,0:T(2,128)(2,1)S(1)}, u32[]{:S(2)}, u32[]{:S(2)}) collective-permute-start(bf16[1,4096]{1,0:T(2,128)(2,1)} %query_ref.1), channel_id=1, source_target_pairs={{0,12},{1,17},{2,14},{3,19},{4,8},{5,21},{6,10},{7,23},{8,4},{9,25... | collective-permute-start | bytes 24584 | tf_op jit(solution)/shard_map/ppermute | solution.py:308
  6.5 1.5 %collective-permute-start.3 = (bf16[1,4096]{1,0:T(2,128)(2,1)}, bf16[1,4096]{1,0:T(2,128)(2,1)S(1)}, u32[]{:S(2)}, u32[]{:S(2)}) collective-permute-start(bf16[1,4096]{1,0:T(2,128)(2,1)} %query_ref.1), channel_id=1, source_target_pairs={{0,4},{1,25},{2,6},{3,27},{4,0},{5,29},{6,2},{7,31},{8,12},{9,17},... | collective-permute-start | bytes 24584 | tf_op jit(solution)/shard_map/ppermute | solution.py:308
  8.0 0.4 %collective-permute-start.2 = (bf16[1,4096]{1,0:T(2,128)(2,1)}, bf16[1,4096]{1,0:T(2,128)(2,1)S(1)}, u32[]{:S(2)}, u32[]{:S(2)}) collective-permute-start(bf16[1,4096]{1,0:T(2,128)(2,1)} %query_ref.1), channel_id=1, source_target_pairs={{0,8},{1,9},{2,10},{3,11},{4,12},{5,13},{6,14},{7,15},{8,0},{9,1},... | collective-permute-start | bytes 24584 | tf_op jit(solution)/shard_map/ppermute | solution.py:310
  9.1 1.8 %shard_map.64 = (bf16[1,32,128]{2,1,0:T(8,128)(2,1)S(1)}, s32[8,128]{1,0:T(8,128)S(1)}, bf16[256,512]{1,0:T(8,128)(2,1)S(1)}, bf16[256,512]{1,0:T(8,128)(2,1)S(1...) custom-call(bf16[1,4096]{1,0:T(2,128)(2,1)} %query_ref.1, s32[1,1]{1,0:T(1,128)} %bitcast.6.lengths_ref, ...), custom_call_target="tpu_custom_call" | custom-call | tf_op jit(solution)/shard_map/pallas_call | solution.py:278
  10.9 0.0 collective-permute-done.1.refs_1_
  10.9 0.0 collective-permute-done.refs_0_
  10.9 0.0 collective-permute-done.3.refs_3_
  10.9 1.0 %collective-permute-done.2.refs_2_ = bf16[1,4096]{1,0:T(2,128)(2,1)S(1)} collective-permute-done((bf16[1,4096]{1,0:T(2,128)(2,1)}, bf16[1,4096]{1,0:T(2,128)(2,1)S(1)}, u32[]{:S(2)}, u32[]{:S(2)}) %collective-permute-start.2) | collective-permute-done | bytes 8224 | tf_op jit(solution)/shard_map/ppermute | solution.py:310
  12.0 0.1 collective-permute-start.4
  12.1 0.5 %shard_map.66 = (f32[4,8,128]{2,1,0:T(8,128)S(1)}, f32[4,8,128]{2,1,0:T(8,128)S(1)}, f32[2,8,128]{2,1,0:T(8,128)S(1)}) custom-call(s32[8,128]{1,0:T(8,128)S(1)} %get-tuple-element.18.length_ref, bf16[2,32,128]{2,1,0:T(8,128)(2,1)S(1)} %get-tuple-element.20.query_ref.refs_0_, bf16[256,512]{1,0:T(8,128)(2,1)S(1)} %get-tuple-element.21.own_key_ref, ...), custom_call_target="tpu_custom_call" | custom-call | tf_op jit(solution)/shard_map/pallas_call | solution.py:333
  12.6 0.7 %collective-permute-done.4.refs_2_ = bf16[3,32,128]{2,1,0:T(8,128)(2,1)S(1)} collective-permute-done((bf16[3,32,128]{2,1,0:T(8,128)(2,1)S(1)}, bf16[3,32,128]{2,1,0:T(8,128)(2,1)S(1)}, u32[]{:S(2)}, u32[]{:S(2)}) %collective-permute-start.4) | collective-permute-done | bytes 24608 | tf_op jit(solution)/shard_map/ppermute | solution.py:321
  13.3 0.8 %shard_map.67 = f32[320,128]{1,0:T(8,128)S(1)} custom-call(bf16[512,1024]{1,0:T(8,128)(2,1)S(1)} %get-tuple-element.16.key_ref, bf16[1024,512]{1,0:T(8,128)(2,1)S(1)} %get-tuple-element.17.value_ref, f32[4,8,128]{2,1,0:T(8,128)S(1)} %get-tuple-element.23.own_ref, f32[4,8,128]{2,1,0:T(8,128)S(1)} %get-tuple-element.24.own_sums_ref, ...), custom_call_target="tpu_custom_call" | custom-call | tf_op jit(solution)/shard_map/pallas_call | solution.py:345
  14.1 9.3 %all_to_all.5 = f16[32,5,2,128]{3,2,1,0:T(2,128)(2,1)S(1)} all-to-all(f16[32,5,2,128]{3,2,1,0:T(2,128)(2,1)S(1)} %bitcast.7), channel_id=1, replica_groups=mesh['seq'=8,'grp'=4] {'seq','grp'}, dimensions={0} | all-to-all | bytes 163840 | tf_op jit(solution)/shard_map/all_to_all | solution.py:354
  23.4 0.9 %shard_map.68 = bf16[1,1024]{1,0:T(2,128)(2,1)} custom-call(f32[320,128]{1,0:T(8,128)S(1)} %convert.1.parts_ref), custom_call_target="tpu_custom_call" | custom-call | tf_op jit(solution)/shard_map/pallas_call | solution.py:356
  (3 shorter events, 0.1 us)
Async XLA Ops:
  0.0 10.9 %collective-permute-start.1 = (bf16[1,4096]{1,0:T(2,128)(2,1)}, bf16[1,4096]{1,0:T(2,128)(2,1)S(1)}, u32[]{:S(2)}, u32[]{:S(2)}) collective-permute-start(bf16[1,4096]{1,0:T(2,128)(2,1)} %query_ref.1), channel_id=1, source_target_pairs={{0,20},{1,29},{2,22},{3,31},{4,16},{5,25},{6,18},{7,27},{8,28},{9,... | collective-permute-start | bytes 24584 | tf_op jit(solution)/shard_map/ppermute | solution.py:308
  5.0 5.9 %collective-permute-start = (bf16[1,4096]{1,0:T(2,128)(2,1)}, bf16[1,4096]{1,0:T(2,128)(2,1)S(1)}, u32[]{:S(2)}, u32[]{:S(2)}) collective-permute-start(bf16[1,4096]{1,0:T(2,128)(2,1)} %query_ref.1), channel_id=1, source_target_pairs={{0,12},{1,17},{2,14},{3,19},{4,8},{5,21},{6,10},{7,23},{8,4},{9,25... | collective-permute-start | bytes 24584 | tf_op jit(solution)/shard_map/ppermute | solution.py:308
  6.5 4.4 %collective-permute-start.3 = (bf16[1,4096]{1,0:T(2,128)(2,1)}, bf16[1,4096]{1,0:T(2,128)(2,1)S(1)}, u32[]{:S(2)}, u32[]{:S(2)}) collective-permute-start(bf16[1,4096]{1,0:T(2,128)(2,1)} %query_ref.1), channel_id=1, source_target_pairs={{0,4},{1,25},{2,6},{3,27},{4,0},{5,29},{6,2},{7,31},{8,12},{9,17},... | collective-permute-start | bytes 24584 | tf_op jit(solution)/shard_map/ppermute | solution.py:308
  8.0 3.9 %collective-permute-start.2 = (bf16[1,4096]{1,0:T(2,128)(2,1)}, bf16[1,4096]{1,0:T(2,128)(2,1)S(1)}, u32[]{:S(2)}, u32[]{:S(2)}) collective-permute-start(bf16[1,4096]{1,0:T(2,128)(2,1)} %query_ref.1), channel_id=1, source_target_pairs={{0,8},{1,9},{2,10},{3,11},{4,12},{5,13},{6,14},{7,15},{8,0},{9,1},... | collective-permute-start | bytes 24584 | tf_op jit(solution)/shard_map/ppermute | solution.py:310
  12.0 1.3 %collective-permute-start.4 = (bf16[3,32,128]{2,1,0:T(8,128)(2,1)S(1)}, bf16[3,32,128]{2,1,0:T(8,128)(2,1)S(1)}, u32[]{:S(2)}, u32[]{:S(2)}) collective-permute-start(bf16[3,32,128]{2,1,0:T(8,128)(2,1)S(1)} %get-tuple-element.26.refs_1_), channel_id=1, source_target_pairs={{0,1},{1,0},{2,3},{3,2},{4,5},{5,4},{6,7},{7,6},{8,9},{9,8},{10,11... | collective-permute-start | bytes 73736 | tf_op jit(solution)/shard_map/ppermute | solution.py:321
